TPU v7x, 512 devices: a whole 4x8x8 slice. The times are simulated.
512 devices in a mesh: dp: 8 (over y_hi, x), ctx: 16 (over z, core), exp: 4 (over y_lo).
Axes of the slice: x: 4, y: 8 (y_hi: 2, y_lo: 4; y = y_hi * 4 + y_lo), z: 8, core: 2. Of those that a mesh axis runs over, the one named last changes fastest.
Arguments:
- queries: bfloat16 [16384, 4096], P(('dp', 'ctx'), 'exp'), may hold values from -4 to 4
- saved_key_rows: bfloat16 [16384, 256], P(('dp', 'ctx'), 'exp'), may hold values from -4 to 4
- saved_value_rows: bfloat16 [16384, 256], P(('dp', 'ctx'), 'exp'), may hold values from -6 to 6
- attn_out: bfloat16 [16384, 4096], P(('dp', 'ctx'), 'exp'), may hold values from -6 to 6
- log_sum_norm: float32 [64, 16384], P('exp', ('dp', 'ctx')), may hold values from 4 to 7
- grad_out: bfloat16 [16384, 4096], P(('dp', 'ctx'), 'exp'), may hold values from -6 to 6
- routes: int32 [16384, 2], P(('dp', 'ctx')), may hold values from 0 to 15, all different within a row; in each aligned block of 128 rows (0 to 127, 128 to 255, ...) at most 32 rows name the same one
- gates: float32 [16384, 2], P(('dp', 'ctx')), may hold values from 0.1 to 1
- expert_in: bfloat16 [8, 16, 512, 4096], P('dp', 'ctx', None, 'exp'), may hold values from -0.09375 to 0.09375
- hidden_grad: bfloat16 [8, 16, 512, 1536], P('dp', 'ctx'), may hold values from -6 to 6
- up_weight: bfloat16 [16, 1536, 4096], P('ctx', 'dp', 'exp'), may hold values from -0.15625 to 0.15625
Outputs:
- grad_hidden: bfloat16 [16384, 4096], P(('dp', 'ctx'), 'exp')
- query_gradient: bfloat16 [16384, 4096], P(('dp', 'ctx'), 'exp')
- key_gradient: bfloat16 [16384, 256], P(('dp', 'ctx'), 'exp')
- value_gradient: bfloat16 [16384, 256], P(('dp', 'ctx'), 'exp')
- grad_up: bfloat16 [16, 1536, 4096], P('ctx', 'dp', 'exp')
Inputs may be any that keep to these rules, and one draw needn't show every extreme that they name: Each token names 2 different experts. Among the tokens of one device (an aligned block of 128 rows) no expert is named by more than 32 routes; some expert is named by exactly 32 routes in some blocks.
All inputs are finite; a program needn't handle non-finite values.
Results may differ from a plain program's by a relative error of at most 0.015.
Values may be sent and summed in bfloat16 or wider, within the bound.
No kernel may reach another device: no remote copies, remote signals or barrier semaphores. Data moves between devices by JAX's collectives and lax.ppermute only.
A program may use at most 128 MiB of HBM per device.

v0:
```python
import jax
import jax.numpy as jnp
from jax import lax
from jax.sharding import PartitionSpec as P

HEAD_WIDTH = 64


def from_behind(shard, axis, by):
    devices = lax.axis_size(axis)
    return lax.ppermute(shard, axis, [(i, (i + by) % devices) for i in range(devices)])


def slot_places(route_rows, experts):
    flat_routes = route_rows.reshape(-1)
    onehot = (flat_routes[:, None] == jnp.arange(experts, dtype=jnp.int32)[None, :]).astype(
        jnp.int32
    )
    before = jnp.cumsum(onehot, axis=0) - onehot
    return (flat_routes, jnp.sum(before * onehot, axis=1))


def block_grads(
    query_rows,
    grad_heads,
    norm_row_values,
    row_delta,
    key_block,
    value_block,
    query_start,
    key_start,
):
    score_scale = HEAD_WIDTH ** (-0.5)
    scores = (
        jnp.einsum("qgc,kc->gqk", query_rows, key_block, preferred_element_type=jnp.float32)
        * score_scale
    )
    query_pos = query_start + jnp.arange(query_rows.shape[0], dtype=jnp.int32)
    key_pos = key_start + jnp.arange(key_block.shape[0], dtype=jnp.int32)
    allowed = key_pos[None, :] <= query_pos[:, None]
    attend = jnp.where(allowed[None], jnp.exp(scores - norm_row_values[:, :, None]), 0.0)
    value_grad_rows = jnp.einsum(
        "gqk,qgc->kc", attend.astype(jnp.bfloat16), grad_heads, preferred_element_type=jnp.float32
    )
    prob_grad = jnp.einsum(
        "qgc,kc->gqk", grad_heads, value_block, preferred_element_type=jnp.float32
    )
    score_grad = (attend * (prob_grad - row_delta[:, :, None])).astype(jnp.bfloat16)
    query_grad_rows = (
        jnp.einsum("gqk,kc->qgc", score_grad, key_block, preferred_element_type=jnp.float32)
        * score_scale
    )
    key_grad_rows = (
        jnp.einsum("gqk,qgc->kc", score_grad, query_rows, preferred_element_type=jnp.float32)
        * score_scale
    )
    return (query_grad_rows, key_grad_rows, value_grad_rows)


def body(
    queries,
    saved_key_rows,
    saved_value_rows,
    attn_out,
    log_sum_norm,
    grad_out,
    routes,
    gates,
    expert_in,
    hidden_grad,
    up_weight,
):
    cycle_size = lax.axis_size("ctx")
    cycle_place = lax.axis_index("ctx")
    rows_dev = queries.shape[0]
    top_count = routes.shape[1]
    slot_rows = hidden_grad.shape[2]
    capacity = slot_rows // cycle_size
    width_dev = grad_out.shape[1]
    flat_routes, places = slot_places(routes, cycle_size)
    slot_grads = hidden_grad[0, 0]
    inputs_dev = expert_in[0, 0]
    columns = slot_grads
    back_rows = jnp.dot(
        columns,
        lax.all_gather(up_weight[0], "dp", axis=0, tiled=True),
        preferred_element_type=jnp.float32,
    )
    grad_up = None
    columns = slot_grads
    summed = lax.psum_scatter(
        lax.dot_general(
            columns, inputs_dev, (((0,), (0,)), ((), ())), preferred_element_type=jnp.float32
        ).astype(jnp.bfloat16),
        "dp",
        scatter_dimension=0,
        tiled=True,
    )
    grad_up = summed.reshape(up_weight.shape)
    returned = lax.all_to_all(
        back_rows.astype(jnp.bfloat16).reshape(cycle_size, capacity, width_dev),
        "ctx",
        split_axis=0,
        concat_axis=0,
        tiled=True,
    )
    picked = returned.reshape(cycle_size * capacity, width_dev)[flat_routes * capacity + places]
    weighted = (
        picked.astype(jnp.float32).reshape(rows_dev, top_count, width_dev) * gates[:, :, None]
    )
    grad_hidden = (grad_out.astype(jnp.float32) + jnp.sum(weighted, axis=1)).astype(jnp.bfloat16)
    group_width = queries.shape[1] // HEAD_WIDTH
    query_heads = queries.reshape(rows_dev, group_width, HEAD_WIDTH)
    grad_heads = grad_hidden.reshape(rows_dev, group_width, HEAD_WIDTH)
    row_delta = jnp.sum(
        grad_heads.astype(jnp.float32)
        * attn_out.reshape(rows_dev, group_width, HEAD_WIDTH).astype(jnp.float32),
        axis=2,
    ).T
    query_start = cycle_place * rows_dev
    zeros_query = jnp.zeros((rows_dev, group_width, HEAD_WIDTH), jnp.float32)
    zeros_key = jnp.zeros((rows_dev, HEAD_WIDTH), jnp.float32)

    def cycle_visit(cycle_step, cycle_state):
        key_block, value_block, key_acc, value_acc, query_acc = cycle_state
        source = (cycle_place - cycle_step) % cycle_size

        def active(query_total, key_total, value_total):
            parts = block_grads(
                query_heads,
                grad_heads,
                log_sum_norm,
                row_delta,
                key_block.astype(jnp.bfloat16),
                value_block.astype(jnp.bfloat16),
                query_start,
                source * rows_dev,
            )
            return (query_total + parts[0], key_total + parts[1], value_total + parts[2])

        def skipped(query_total, key_total, value_total):
            return (query_total, key_total, value_total)

        query_acc, key_acc, value_acc = lax.cond(
            source <= cycle_place, active, skipped, query_acc, key_acc, value_acc
        )
        key_block, value_block, key_acc, value_acc = from_behind(
            (key_block, value_block, key_acc, value_acc), "ctx", 1
        )
        return (key_block, value_block, key_acc, value_acc, query_acc)

    cycle_state = lax.fori_loop(
        0,
        cycle_size,
        cycle_visit,
        (
            saved_key_rows.astype(jnp.float32),
            saved_value_rows.astype(jnp.float32),
            zeros_key,
            zeros_key,
            zeros_query,
        ),
    )
    key_acc, value_acc, query_acc = (cycle_state[2], cycle_state[3], cycle_state[4])
    query_gradient = query_acc.reshape(rows_dev, group_width * HEAD_WIDTH).astype(jnp.bfloat16)
    return (
        grad_hidden,
        query_gradient,
        key_acc.astype(jnp.bfloat16),
        value_acc.astype(jnp.bfloat16),
        grad_up,
    )


def solution(mesh):
    placed = (
        P(("dp", "ctx"), "exp"),
        P(("dp", "ctx"), "exp"),
        P(("dp", "ctx"), "exp"),
        P(("dp", "ctx"), "exp"),
        P("exp", ("dp", "ctx")),
        P(("dp", "ctx"), "exp"),
        P(("dp", "ctx"), None),
        P(("dp", "ctx"), None),
        P("dp", "ctx", None, "exp"),
        P("dp", "ctx", None, None),
        P("ctx", "dp", "exp"),
    )
    return jax.shard_map(
        body,
        mesh=mesh,
        in_specs=placed,
        out_specs=(
            P(("dp", "ctx"), "exp"),
            P(("dp", "ctx"), "exp"),
            P(("dp", "ctx"), "exp"),
            P(("dp", "ctx"), "exp"),
            P("ctx", "dp", "exp"),
        ),
        check_vma=False,
    )
```

profile of v0, /device:TPU:1, one launch (start us, length us, event | category | flops | bytes accessed | tf_op | source)
XLA Modules:
  0.0 258.7 jit_solution(7837791762556449529)
XLA Ops:
  8.6 4.7 %convolution_convert_fusion = bf16[1536,1024]{1,0:T(8,128)(2,1)} fusion(bf16[1,1,512,1536]{3,2,1,0:T(8,128)(2,1)S(1)} %copy-done, bf16[1,1,512,1024]{3,2,1,0:T(8,128)(2,1)} %param.23), kind=kOutput, calls=%fused_computation.28 | convolution fusion | flops 1612185600 | bytes 5767168 | tf_op jit(solution)/shard_map/dot_general | solution.py:92
  13.3 95.9 %all-gather.3.cloned.1.call-done = bf16[1,1536,1024]{2,1,0:T(8,128)(2,1)} async-done(((bf16[1,192,1024]{2,1,0:T(8,128)(2,1)}), bf16[1,1536,1024]{2,1,0:T(8,128)(2,1)}) %all-gather.3.cloned.1.call-update) | async-done | bytes 3145744 | tf_op jit(solution)/shard_map/all_gather | solution.py:86
  109.2 4.7 %fusion.23 = bf16[512,1024]{1,0:T(8,128)(2,1)} fusion(bf16[1,1536,1024]{2,1,0:T(8,128)(2,1)} %all-gather.3.cloned.1.call-done, bf16[1,1,512,1536]{3,2,1,0:T(8,128)(2,1)S(1)} %copy-done), kind=kOutput, calls=%fused_computation.33 | convolution fusion | flops 1611137024 | bytes 5767168 | tf_op jit(solution)/shard_map/dot_general | solution.py:84
  113.9 6.8 %all-to-all-start = ((bf16[16,32,1024]{2,1,0:T(8,128)(2,1)}), bf16[16,32,1024]{2,1,0:T(8,128)(2,1)S(1)}, u32[]{:S(2)}, u32[]{:S(2)}) async-start(bf16[16,32,1024]{2,1,0:T(8,128)(2,1)} %bitcast.95), calls=%async_computation | async-start | bytes 2097152 | tf_op jit(solution)/shard_map/all_to_all | solution.py:100
  122.5 0.8 copy.46
  123.5 25.2 %all-to-all-done = bf16[16,32,1024]{2,1,0:T(8,128)(2,1)S(1)} async-done(((bf16[16,32,1024]{2,1,0:T(8,128)(2,1)}), bf16[16,32,1024]{2,1,0:T(8,128)(2,1)S(1)}, u32[]{:S(2)}, u32[]{:S(2)}) %all-to-all-start) | async-done | bytes 1048608 | tf_op jit(solution)/shard_map/all_to_all | solution.py:100
  148.7 1.2 gather_fusion
  150.5 1.3 multiply_reduce_fusion
  151.9 1.0 add_convert_fusion
  153.6 96.1 %while.23 = (s32[]{:T(128)}, bf16[128,64]{0,1:T(8,128)(2,1)S(1)}, bf16[128,64]{0,1:T(8,128)(2,1)S(1)}, f32[128,64]{0,1:T(8,128)S(1)}, f32[128,64]{0,1:T(8,128)S(...) while((s32[]{:T(128)}, bf16[128,64]{0,1:T(8,128)(2,1)S(1)}, ...), condition=%wide.region_8.9_spmd, body=%wide.region_5.8_spmd.sunk | while | flops 169910544 | bytes 7637600 | solution.py:152
  153.6 1.6 conditional.2
  155.4 1.2 collective-permute-start.1
  157.4 1.6 conditional.2
  159.1 2.3 collective-permute-start.2
  161.4 2.0 collective-permute-start
  164.7 3.8 %collective-permute-start.2 = (f32[128,64]{0,1:T(8,128)S(1)}, f32[128,64]{0,1:T(8,128)S(1)}, u32[]{:S(2)}, u32[]{:S(2)}) collective-permute-start(f32[128,64]{0,1:T(8,128)S(1)} %get-tuple-element.468), channel_id=1, source_target_pairs={{0,4},{4,8},{8,12},{12,16},{16,20},{20,24},{24,28},{28,32},{32,36}... | collective-permute-start | bytes 98312 | tf_op jit(solution)/shard_map/while/body/eval_jaxpr/ppermute | solution.py:11
  168.6 1.0 collective-permute-start
  170.7 2.3 collective-permute-start.2
  173.0 1.9 collective-permute-start.3
  174.9 2.2 collective-permute-start
  177.1 0.8 collective-permute-done
  178.2 2.2 collective-permute-start.2
  180.4 3.5 %collective-permute-start = (bf16[128,64]{0,1:T(8,128)(2,1)S(1)}, bf16[128,64]{0,1:T(8,128)(2,1)S(1)}, u32[]{:S(2)}, u32[]{:S(2)}) collective-permute-start(bf16[128,64]{0,1:T(8,128)(2,1)S(1)} %copy.66), channel_id=1, source_target_pairs={{0,4},{4,8},{8,12},{12,16},{16,20},{20,24},{24,28},{28,32},{32,36}... | collective-permute-start | bytes 49160 | tf_op jit(solution)/shard_map/while/body/eval_jaxpr/ppermute | solution.py:11
  185.2 2.2 collective-permute-start.2
  187.3 1.9 collective-permute-start
  189.2 1.4 collective-permute-start.1
  190.7 0.8 collective-permute-done.1
  191.5 2.3 collective-permute-start.2
  194.0 2.2 collective-permute-start
  197.4 3.2 %collective-permute-start.2 = (f32[128,64]{0,1:T(8,128)S(1)}, f32[128,64]{0,1:T(8,128)S(1)}, u32[]{:S(2)}, u32[]{:S(2)}) collective-permute-start(f32[128,64]{0,1:T(8,128)S(1)} %get-tuple-element.468), channel_id=1, source_target_pairs={{0,4},{4,8},{8,12},{12,16},{16,20},{20,24},{24,28},{28,32},{32,36}... | collective-permute-start | bytes 98312 | tf_op jit(solution)/shard_map/while/body/eval_jaxpr/ppermute | solution.py:11
  200.9 2.2 collective-permute-start
  204.3 2.2 collective-permute-start.2
  206.5 3.0 %collective-permute-start = (bf16[128,64]{0,1:T(8,128)(2,1)S(1)}, bf16[128,64]{0,1:T(8,128)(2,1)S(1)}, u32[]{:S(2)}, u32[]{:S(2)}) collective-permute-start(bf16[128,64]{0,1:T(8,128)(2,1)S(1)} %copy.66), channel_id=1, source_target_pairs={{0,4},{4,8},{8,12},{12,16},{16,20},{20,24},{24,28},{28,32},{32,36}... | collective-permute-start | bytes 49160 | tf_op jit(solution)/shard_map/while/body/eval_jaxpr/ppermute | solution.py:11
  210.7 2.3 collective-permute-start.2
  213.1 3.2 %collective-permute-start = (bf16[128,64]{0,1:T(8,128)(2,1)S(1)}, bf16[128,64]{0,1:T(8,128)(2,1)S(1)}, u32[]{:S(2)}, u32[]{:S(2)}) collective-permute-start(bf16[128,64]{0,1:T(8,128)(2,1)S(1)} %copy.66), channel_id=1, source_target_pairs={{0,4},{4,8},{8,12},{12,16},{16,20},{20,24},{24,28},{28,32},{32,36}... | collective-permute-start | bytes 49160 | tf_op jit(solution)/shard_map/while/body/eval_jaxpr/ppermute | solution.py:11
  217.6 2.3 collective-permute-start.2
  220.1 2.2 collective-permute-start
  223.4 2.2 collective-permute-start.2
  225.6 1.9 collective-permute-start
  228.7 2.2 collective-permute-start.2
  230.9 1.9 collective-permute-start
  233.9 2.2 collective-permute-start.2
  236.1 1.9 collective-permute-start
  239.2 2.2 collective-permute-start.2
  241.4 1.9 collective-permute-start
  244.4 2.2 collective-permute-start.2
  246.6 1.9 collective-permute-start
  249.7 0.9 copy.47
  (235 shorter events, 27.0 us)
Async XLA Ops:
  7.2 102.0 %all-gather.3.cloned.1.call-start = ((), (), s32[]{:S(2)}) async-start(), calls=%async_computation.3 | async-start | bytes 3538944 | tf_op jit(solution)/shard_map/all_gather | solution.py:86
  7.9 243.9 %reduce-scatter.2.cloned.1.call-start = ((), (), s32[]{:S(2)}) async-start(), calls=%async_computation.2 | async-start | bytes 3538944 | tf_op jit(solution)/shard_map/reduce_scatter | solution.py:91
  113.9 34.8 %all-to-all-start = ((bf16[16,32,1024]{2,1,0:T(8,128)(2,1)}), bf16[16,32,1024]{2,1,0:T(8,128)(2,1)S(1)}, u32[]{:S(2)}, u32[]{:S(2)}) async-start(bf16[16,32,1024]{2,1,0:T(8,128)(2,1)} %bitcast.95), calls=%async_computation | async-start | bytes 2097152 | tf_op jit(solution)/shard_map/all_to_all | solution.py:100
  155.4 2.1 collective-permute-start.1
  159.1 4.4 %collective-permute-start.2 = (f32[128,64]{0,1:T(8,128)S(1)}, f32[128,64]{0,1:T(8,128)S(1)}, u32[]{:S(2)}, u32[]{:S(2)}) collective-permute-start(f32[128,64]{0,1:T(8,128)S(1)} %get-tuple-element.468), channel_id=1, source_target_pairs={{0,4},{4,8},{8,12},{12,16},{16,20},{20,24},{24,28},{28,32},{32,36}... | collective-permute-start | bytes 98312 | tf_op jit(solution)/shard_map/while/body/eval_jaxpr/ppermute | solution.py:11
  161.4 2.1 collective-permute-start.3
  161.4 2.9 %collective-permute-start = (bf16[128,64]{0,1:T(8,128)(2,1)S(1)}, bf16[128,64]{0,1:T(8,128)(2,1)S(1)}, u32[]{:S(2)}, u32[]{:S(2)}) collective-permute-start(bf16[128,64]{0,1:T(8,128)(2,1)S(1)} %copy.66), channel_id=1, source_target_pairs={{0,4},{4,8},{8,12},{12,16},{16,20},{20,24},{24,28},{28,32},{32,36}... | collective-permute-start | bytes 49160 | tf_op jit(solution)/shard_map/while/body/eval_jaxpr/ppermute | solution.py:11
  164.7 5.2 %collective-permute-start.2 = (f32[128,64]{0,1:T(8,128)S(1)}, f32[128,64]{0,1:T(8,128)S(1)}, u32[]{:S(2)}, u32[]{:S(2)}) collective-permute-start(f32[128,64]{0,1:T(8,128)S(1)} %get-tuple-element.468), channel_id=1, source_target_pairs={{0,4},{4,8},{8,12},{12,16},{16,20},{20,24},{24,28},{28,32},{32,36}... | collective-permute-start | bytes 98312 | tf_op jit(solution)/shard_map/while/body/eval_jaxpr/ppermute | solution.py:11
  170.7 6.4 %collective-permute-start.2 = (f32[128,64]{0,1:T(8,128)S(1)}, f32[128,64]{0,1:T(8,128)S(1)}, u32[]{:S(2)}, u32[]{:S(2)}) collective-permute-start(f32[128,64]{0,1:T(8,128)S(1)} %get-tuple-element.468), channel_id=1, source_target_pairs={{0,4},{4,8},{8,12},{12,16},{16,20},{20,24},{24,28},{28,32},{32,36}... | collective-permute-start | bytes 98312 | tf_op jit(solution)/shard_map/while/body/eval_jaxpr/ppermute | solution.py:11
  173.0 4.1 %collective-permute-start.3 = (f32[128,64]{0,1:T(8,128)S(1)}, f32[128,64]{0,1:T(8,128)S(1)}, u32[]{:S(2)}, u32[]{:S(2)}) collective-permute-start(f32[128,64]{0,1:T(8,128)S(1)} %get-tuple-element.469), channel_id=1, source_target_pairs={{0,4},{4,8},{8,12},{12,16},{16,20},{20,24},{24,28},{28,32},{32,36}... | collective-permute-start | bytes 98312 | tf_op jit(solution)/shard_map/while/body/eval_jaxpr/ppermute | solution.py:11
  174.9 3.0 %collective-permute-start = (bf16[128,64]{0,1:T(8,128)(2,1)S(1)}, bf16[128,64]{0,1:T(8,128)(2,1)S(1)}, u32[]{:S(2)}, u32[]{:S(2)}) collective-permute-start(bf16[128,64]{0,1:T(8,128)(2,1)S(1)} %copy.66), channel_id=1, source_target_pairs={{0,4},{4,8},{8,12},{12,16},{16,20},{20,24},{24,28},{28,32},{32,36}... | collective-permute-start | bytes 49160 | tf_op jit(solution)/shard_map/while/body/eval_jaxpr/ppermute | solution.py:11
  178.2 5.8 %collective-permute-start.2 = (f32[128,64]{0,1:T(8,128)S(1)}, f32[128,64]{0,1:T(8,128)S(1)}, u32[]{:S(2)}, u32[]{:S(2)}) collective-permute-start(f32[128,64]{0,1:T(8,128)S(1)} %get-tuple-element.468), channel_id=1, source_target_pairs={{0,4},{4,8},{8,12},{12,16},{16,20},{20,24},{24,28},{28,32},{32,36}... | collective-permute-start | bytes 98312 | tf_op jit(solution)/shard_map/while/body/eval_jaxpr/ppermute | solution.py:11
  180.4 3.6 %collective-permute-start.3 = (f32[128,64]{0,1:T(8,128)S(1)}, f32[128,64]{0,1:T(8,128)S(1)}, u32[]{:S(2)}, u32[]{:S(2)}) collective-permute-start(f32[128,64]{0,1:T(8,128)S(1)} %get-tuple-element.469), channel_id=1, source_target_pairs={{0,4},{4,8},{8,12},{12,16},{16,20},{20,24},{24,28},{28,32},{32,36}... | collective-permute-start | bytes 98312 | tf_op jit(solution)/shard_map/while/body/eval_jaxpr/ppermute | solution.py:11
  180.4 4.4 %collective-permute-start = (bf16[128,64]{0,1:T(8,128)(2,1)S(1)}, bf16[128,64]{0,1:T(8,128)(2,1)S(1)}, u32[]{:S(2)}, u32[]{:S(2)}) collective-permute-start(bf16[128,64]{0,1:T(8,128)(2,1)S(1)} %copy.66), channel_id=1, source_target_pairs={{0,4},{4,8},{8,12},{12,16},{16,20},{20,24},{24,28},{28,32},{32,36}... | collective-permute-start | bytes 49160 | tf_op jit(solution)/shard_map/while/body/eval_jaxpr/ppermute | solution.py:11
  185.2 5.5 %collective-permute-start.2 = (f32[128,64]{0,1:T(8,128)S(1)}, f32[128,64]{0,1:T(8,128)S(1)}, u32[]{:S(2)}, u32[]{:S(2)}) collective-permute-start(f32[128,64]{0,1:T(8,128)S(1)} %get-tuple-element.468), channel_id=1, source_target_pairs={{0,4},{4,8},{8,12},{12,16},{16,20},{20,24},{24,28},{28,32},{32,36}... | collective-permute-start | bytes 98312 | tf_op jit(solution)/shard_map/while/body/eval_jaxpr/ppermute | solution.py:11
  187.3 3.3 %collective-permute-start.3 = (f32[128,64]{0,1:T(8,128)S(1)}, f32[128,64]{0,1:T(8,128)S(1)}, u32[]{:S(2)}, u32[]{:S(2)}) collective-permute-start(f32[128,64]{0,1:T(8,128)S(1)} %get-tuple-element.469), channel_id=1, source_target_pairs={{0,4},{4,8},{8,12},{12,16},{16,20},{20,24},{24,28},{28,32},{32,36}... | collective-permute-start | bytes 98312 | tf_op jit(solution)/shard_map/while/body/eval_jaxpr/ppermute | solution.py:11
  187.3 3.3 %collective-permute-start = (bf16[128,64]{0,1:T(8,128)(2,1)S(1)}, bf16[128,64]{0,1:T(8,128)(2,1)S(1)}, u32[]{:S(2)}, u32[]{:S(2)}) collective-permute-start(bf16[128,64]{0,1:T(8,128)(2,1)S(1)} %copy.66), channel_id=1, source_target_pairs={{0,4},{4,8},{8,12},{12,16},{16,20},{20,24},{24,28},{28,32},{32,36}... | collective-permute-start | bytes 49160 | tf_op jit(solution)/shard_map/while/body/eval_jaxpr/ppermute | solution.py:11
  189.2 2.3 collective-permute-start.1
  191.5 4.7 %collective-permute-start.2 = (f32[128,64]{0,1:T(8,128)S(1)}, f32[128,64]{0,1:T(8,128)S(1)}, u32[]{:S(2)}, u32[]{:S(2)}) collective-permute-start(f32[128,64]{0,1:T(8,128)S(1)} %get-tuple-element.468), channel_id=1, source_target_pairs={{0,4},{4,8},{8,12},{12,16},{16,20},{20,24},{24,28},{28,32},{32,36}... | collective-permute-start | bytes 98312 | tf_op jit(solution)/shard_map/while/body/eval_jaxpr/ppermute | solution.py:11
  193.8 2.4 collective-permute-start.3
  194.0 3.0 %collective-permute-start = (bf16[128,64]{0,1:T(8,128)(2,1)S(1)}, bf16[128,64]{0,1:T(8,128)(2,1)S(1)}, u32[]{:S(2)}, u32[]{:S(2)}) collective-permute-start(bf16[128,64]{0,1:T(8,128)(2,1)S(1)} %copy.66), channel_id=1, source_target_pairs={{0,4},{4,8},{8,12},{12,16},{16,20},{20,24},{24,28},{28,32},{32,36}... | collective-permute-start | bytes 49160 | tf_op jit(solution)/shard_map/while/body/eval_jaxpr/ppermute | solution.py:11
  197.4 5.8 %collective-permute-start.2 = (f32[128,64]{0,1:T(8,128)S(1)}, f32[128,64]{0,1:T(8,128)S(1)}, u32[]{:S(2)}, u32[]{:S(2)}) collective-permute-start(f32[128,64]{0,1:T(8,128)S(1)} %get-tuple-element.468), channel_id=1, source_target_pairs={{0,4},{4,8},{8,12},{12,16},{16,20},{20,24},{24,28},{28,32},{32,36}... | collective-permute-start | bytes 98312 | tf_op jit(solution)/shard_map/while/body/eval_jaxpr/ppermute | solution.py:11
  200.6 2.6 collective-permute-start.3
  200.9 3.0 %collective-permute-start = (bf16[128,64]{0,1:T(8,128)(2,1)S(1)}, bf16[128,64]{0,1:T(8,128)(2,1)S(1)}, u32[]{:S(2)}, u32[]{:S(2)}) collective-permute-start(bf16[128,64]{0,1:T(8,128)(2,1)S(1)} %copy.66), channel_id=1, source_target_pairs={{0,4},{4,8},{8,12},{12,16},{16,20},{20,24},{24,28},{28,32},{32,36}... | collective-permute-start | bytes 49160 | tf_op jit(solution)/shard_map/while/body/eval_jaxpr/ppermute | solution.py:11
  204.3 5.5 %collective-permute-start.2 = (f32[128,64]{0,1:T(8,128)S(1)}, f32[128,64]{0,1:T(8,128)S(1)}, u32[]{:S(2)}, u32[]{:S(2)}) collective-permute-start(f32[128,64]{0,1:T(8,128)S(1)} %get-tuple-element.468), channel_id=1, source_target_pairs={{0,4},{4,8},{8,12},{12,16},{16,20},{20,24},{24,28},{28,32},{32,36}... | collective-permute-start | bytes 98312 | tf_op jit(solution)/shard_map/while/body/eval_jaxpr/ppermute | solution.py:11
  206.4 3.3 %collective-permute-start.3 = (f32[128,64]{0,1:T(8,128)S(1)}, f32[128,64]{0,1:T(8,128)S(1)}, u32[]{:S(2)}, u32[]{:S(2)}) collective-permute-start(f32[128,64]{0,1:T(8,128)S(1)} %get-tuple-element.469), channel_id=1, source_target_pairs={{0,4},{4,8},{8,12},{12,16},{16,20},{20,24},{24,28},{28,32},{32,36}... | collective-permute-start | bytes 98312 | tf_op jit(solution)/shard_map/while/body/eval_jaxpr/ppermute | solution.py:11
  206.5 3.8 %collective-permute-start = (bf16[128,64]{0,1:T(8,128)(2,1)S(1)}, bf16[128,64]{0,1:T(8,128)(2,1)S(1)}, u32[]{:S(2)}, u32[]{:S(2)}) collective-permute-start(bf16[128,64]{0,1:T(8,128)(2,1)S(1)} %copy.66), channel_id=1, source_target_pairs={{0,4},{4,8},{8,12},{12,16},{16,20},{20,24},{24,28},{28,32},{32,36}... | collective-permute-start | bytes 49160 | tf_op jit(solution)/shard_map/while/body/eval_jaxpr/ppermute | solution.py:11
  210.7 6.1 %collective-permute-start.2 = (f32[128,64]{0,1:T(8,128)S(1)}, f32[128,64]{0,1:T(8,128)S(1)}, u32[]{:S(2)}, u32[]{:S(2)}) collective-permute-start(f32[128,64]{0,1:T(8,128)S(1)} %get-tuple-element.468), channel_id=1, source_target_pairs={{0,4},{4,8},{8,12},{12,16},{16,20},{20,24},{24,28},{28,32},{32,36}... | collective-permute-start | bytes 98312 | tf_op jit(solution)/shard_map/while/body/eval_jaxpr/ppermute | solution.py:11
  213.0 3.8 %collective-permute-start.3 = (f32[128,64]{0,1:T(8,128)S(1)}, f32[128,64]{0,1:T(8,128)S(1)}, u32[]{:S(2)}, u32[]{:S(2)}) collective-permute-start(f32[128,64]{0,1:T(8,128)S(1)} %get-tuple-element.469), channel_id=1, source_target_pairs={{0,4},{4,8},{8,12},{12,16},{16,20},{20,24},{24,28},{28,32},{32,36}... | collective-permute-start | bytes 98312 | tf_op jit(solution)/shard_map/while/body/eval_jaxpr/ppermute | solution.py:11
  213.1 4.1 %collective-permute-start = (bf16[128,64]{0,1:T(8,128)(2,1)S(1)}, bf16[128,64]{0,1:T(8,128)(2,1)S(1)}, u32[]{:S(2)}, u32[]{:S(2)}) collective-permute-start(bf16[128,64]{0,1:T(8,128)(2,1)S(1)} %copy.66), channel_id=1, source_target_pairs={{0,4},{4,8},{8,12},{12,16},{16,20},{20,24},{24,28},{28,32},{32,36}... | collective-permute-start | bytes 49160 | tf_op jit(solution)/shard_map/while/body/eval_jaxpr/ppermute | solution.py:11
  217.6 4.7 %collective-permute-start.2 = (f32[128,64]{0,1:T(8,128)S(1)}, f32[128,64]{0,1:T(8,128)S(1)}, u32[]{:S(2)}, u32[]{:S(2)}) collective-permute-start(f32[128,64]{0,1:T(8,128)S(1)} %get-tuple-element.468), channel_id=1, source_target_pairs={{0,4},{4,8},{8,12},{12,16},{16,20},{20,24},{24,28},{28,32},{32,36}... | collective-permute-start | bytes 98312 | tf_op jit(solution)/shard_map/while/body/eval_jaxpr/ppermute | solution.py:11
  219.9 2.4 collective-permute-start.3
  220.1 3.0 %collective-permute-start = (bf16[128,64]{0,1:T(8,128)(2,1)S(1)}, bf16[128,64]{0,1:T(8,128)(2,1)S(1)}, u32[]{:S(2)}, u32[]{:S(2)}) collective-permute-start(bf16[128,64]{0,1:T(8,128)(2,1)S(1)} %copy.66), channel_id=1, source_target_pairs={{0,4},{4,8},{8,12},{12,16},{16,20},{20,24},{24,28},{28,32},{32,36}... | collective-permute-start | bytes 49160 | tf_op jit(solution)/shard_map/while/body/eval_jaxpr/ppermute | solution.py:11
  223.4 4.1 %collective-permute-start.2 = (f32[128,64]{0,1:T(8,128)S(1)}, f32[128,64]{0,1:T(8,128)S(1)}, u32[]{:S(2)}, u32[]{:S(2)}) collective-permute-start(f32[128,64]{0,1:T(8,128)S(1)} %get-tuple-element.468), channel_id=1, source_target_pairs={{0,4},{4,8},{8,12},{12,16},{16,20},{20,24},{24,28},{28,32},{32,36}... | collective-permute-start | bytes 98312 | tf_op jit(solution)/shard_map/while/body/eval_jaxpr/ppermute | solution.py:11
  225.6 2.0 collective-permute-start.3
  225.6 2.7 %collective-permute-start = (bf16[128,64]{0,1:T(8,128)(2,1)S(1)}, bf16[128,64]{0,1:T(8,128)(2,1)S(1)}, u32[]{:S(2)}, u32[]{:S(2)}) collective-permute-start(bf16[128,64]{0,1:T(8,128)(2,1)S(1)} %copy.66), channel_id=1, source_target_pairs={{0,4},{4,8},{8,12},{12,16},{16,20},{20,24},{24,28},{28,32},{32,36}... | collective-permute-start | bytes 49160 | tf_op jit(solution)/shard_map/while/body/eval_jaxpr/ppermute | solution.py:11
  228.7 4.1 %collective-permute-start.2 = (f32[128,64]{0,1:T(8,128)S(1)}, f32[128,64]{0,1:T(8,128)S(1)}, u32[]{:S(2)}, u32[]{:S(2)}) collective-permute-start(f32[128,64]{0,1:T(8,128)S(1)} %get-tuple-element.468), channel_id=1, source_target_pairs={{0,4},{4,8},{8,12},{12,16},{16,20},{20,24},{24,28},{28,32},{32,36}... | collective-permute-start | bytes 98312 | tf_op jit(solution)/shard_map/while/body/eval_jaxpr/ppermute | solution.py:11
  230.8 2.0 collective-permute-start.3
  230.9 2.7 %collective-permute-start = (bf16[128,64]{0,1:T(8,128)(2,1)S(1)}, bf16[128,64]{0,1:T(8,128)(2,1)S(1)}, u32[]{:S(2)}, u32[]{:S(2)}) collective-permute-start(bf16[128,64]{0,1:T(8,128)(2,1)S(1)} %copy.66), channel_id=1, source_target_pairs={{0,4},{4,8},{8,12},{12,16},{16,20},{20,24},{24,28},{28,32},{32,36}... | collective-permute-start | bytes 49160 | tf_op jit(solution)/shard_map/while/body/eval_jaxpr/ppermute | solution.py:11
  233.9 4.1 %collective-permute-start.2 = (f32[128,64]{0,1:T(8,128)S(1)}, f32[128,64]{0,1:T(8,128)S(1)}, u32[]{:S(2)}, u32[]{:S(2)}) collective-permute-start(f32[128,64]{0,1:T(8,128)S(1)} %get-tuple-element.468), channel_id=1, source_target_pairs={{0,4},{4,8},{8,12},{12,16},{16,20},{20,24},{24,28},{28,32},{32,36}... | collective-permute-start | bytes 98312 | tf_op jit(solution)/shard_map/while/body/eval_jaxpr/ppermute | solution.py:11
  236.1 2.0 collective-permute-start.3
  236.1 2.7 %collective-permute-start = (bf16[128,64]{0,1:T(8,128)(2,1)S(1)}, bf16[128,64]{0,1:T(8,128)(2,1)S(1)}, u32[]{:S(2)}, u32[]{:S(2)}) collective-permute-start(bf16[128,64]{0,1:T(8,128)(2,1)S(1)} %copy.66), channel_id=1, source_target_pairs={{0,4},{4,8},{8,12},{12,16},{16,20},{20,24},{24,28},{28,32},{32,36}... | collective-permute-start | bytes 49160 | tf_op jit(solution)/shard_map/while/body/eval_jaxpr/ppermute | solution.py:11
  239.2 4.1 %collective-permute-start.2 = (f32[128,64]{0,1:T(8,128)S(1)}, f32[128,64]{0,1:T(8,128)S(1)}, u32[]{:S(2)}, u32[]{:S(2)}) collective-permute-start(f32[128,64]{0,1:T(8,128)S(1)} %get-tuple-element.468), channel_id=1, source_target_pairs={{0,4},{4,8},{8,12},{12,16},{16,20},{20,24},{24,28},{28,32},{32,36}... | collective-permute-start | bytes 98312 | tf_op jit(solution)/shard_map/while/body/eval_jaxpr/ppermute | solution.py:11
  241.3 2.0 collective-permute-start.3
  241.4 2.7 %collective-permute-start = (bf16[128,64]{0,1:T(8,128)(2,1)S(1)}, bf16[128,64]{0,1:T(8,128)(2,1)S(1)}, u32[]{:S(2)}, u32[]{:S(2)}) collective-permute-start(bf16[128,64]{0,1:T(8,128)(2,1)S(1)} %copy.66), channel_id=1, source_target_pairs={{0,4},{4,8},{8,12},{12,16},{16,20},{20,24},{24,28},{28,32},{32,36}... | collective-permute-start | bytes 49160 | tf_op jit(solution)/shard_map/while/body/eval_jaxpr/ppermute | solution.py:11
  244.4 4.1 %collective-permute-start.2 = (f32[128,64]{0,1:T(8,128)S(1)}, f32[128,64]{0,1:T(8,128)S(1)}, u32[]{:S(2)}, u32[]{:S(2)}) collective-permute-start(f32[128,64]{0,1:T(8,128)S(1)} %get-tuple-element.468), channel_id=1, source_target_pairs={{0,4},{4,8},{8,12},{12,16},{16,20},{20,24},{24,28},{28,32},{32,36}... | collective-permute-start | bytes 98312 | tf_op jit(solution)/shard_map/while/body/eval_jaxpr/ppermute | solution.py:11
  246.6 2.0 collective-permute-start.3
  246.6 2.7 %collective-permute-start = (bf16[128,64]{0,1:T(8,128)(2,1)S(1)}, bf16[128,64]{0,1:T(8,128)(2,1)S(1)}, u32[]{:S(2)}, u32[]{:S(2)}) collective-permute-start(bf16[128,64]{0,1:T(8,128)(2,1)S(1)} %copy.66), channel_id=1, source_target_pairs={{0,4},{4,8},{8,12},{12,16},{16,20},{20,24},{24,28},{28,32},{32,36}... | collective-permute-start | bytes 49160 | tf_op jit(solution)/shard_map/while/body/eval_jaxpr/ppermute | solution.py:11
  (29 other events, 69.3 us)
Sparse Core Ops, SparseCore 0:
  11.2 97.9 all-gather.2
  114.6 112.5 reduce-scatter.1
where the time goes:
time: 264 us; the launch traced here: 259 us
  waiting for transfers between devices  138 us (52%)
  starting transfers between devices  82.7 us (31%)
  between operations  14.3 us (5%)
  matrix products  12.4 us (5%)
  local copies, waits for them, and re-layouts  6.01 us (2%)
  other arithmetic  4.63 us (2%)
    all_gather x1, waiting for transfers between devices, body(): lax.all_gather(up_weight[0], 'dp', axis=0, tiled=True)  95.9 us
    ppermute x64, starting transfers between devices, from_behind(): lax.ppermute(shard, axis, [(i, (i + by) % devices) for i in range(devices)])  75.8 us
    all_to_all x1, waiting for transfers between devices, body(): lax.all_to_all(back_rows.astype(jnp.bfloat16).reshape(cycle_size, capacit...  25.2 us
    ppermute x64, waiting for transfers between devices, from_behind(): lax.ppermute(shard, axis, [(i, (i + by) % devices) for i in range(devices)])  16.5 us
    all_to_all x1, starting transfers between devices, body(): lax.all_to_all(back_rows.astype(jnp.bfloat16).reshape(cycle_size, capacit...  6.82 us
  transfers between devices with their start and end apart: 67, of which 34 were waited for; matrix products, arithmetic and copies ran while one was open for 9% of the time, Pallas kernels for 0%

commit v1 on v0

v1 whole, which is shorter than its diff:
```python
import functools

import jax
import jax.numpy as jnp
from jax import lax
from jax.experimental import pallas as pl
from jax.experimental.pallas import tpu as pltpu
from jax.sharding import PartitionSpec as P

HEAD_WIDTH = 64
PAIR = 2 * HEAD_WIDTH
KEY_TILE = 256
ROW_TILE = 1024
QUERY_KEY_TILE = 512
QUERY_ROW_TILE = 512
X_RING = 4
F32 = jnp.float32
BF16 = jnp.bfloat16

NT = (((1,), (1,)), ((), ()))
TN = (((0,), (0,)), ((), ()))
LIGHT = pl.CostEstimate(flops=1 << 20, bytes_accessed=1 << 16, transcendentals=0)
X_GROUPS = [[0, 1, 2, 3], [4, 5, 6, 7]]


def other_y(shard):
    return lax.ppermute(shard, "dp", [(i, (i + X_RING) % (2 * X_RING)) for i in range(2 * X_RING)])


def along_x(shard, by):
    order = [(i, i // X_RING * X_RING + (i + by) % X_RING) for i in range(2 * X_RING)]
    return lax.ppermute(shard, "dp", order)


def run_copies(pairs, sems):
    copies = [pltpu.make_async_copy(src, dst, sems.at[i]) for i, (src, dst) in enumerate(pairs)]
    for copy in copies:
        copy.start()
    return copies


def repeat_kernel(shard_ref, out_ref):
    rows = shard_ref.shape[0]
    for i in range(X_RING):
        out_ref[i * rows : (i + 1) * rows, :] = shard_ref[...]


def repeated(shard):
    vmem = pl.BlockSpec(memory_space=pltpu.VMEM)
    return pl.pallas_call(
        repeat_kernel,
        out_shape=jax.ShapeDtypeStruct((X_RING * shard.shape[0], shard.shape[1]), shard.dtype),
        in_specs=[vmem],
        out_specs=vmem,
        cost_estimate=LIGHT,
        name="repeat",
    )(shard)


def over_x(shard):
    return lax.all_to_all(shard, "dp", 0, 0, tiled=True, axis_index_groups=X_GROUPS)


def back_kernel(line_ref, grads_ref, near_ref, far_ref, out_ref, grads, weight, sems):
    y = line_ref[0] // X_RING
    half = near_ref.shape[0]
    pairs = [(grads_ref, grads)]
    for ref, part in ((near_ref, y), (far_ref, 1 - y)):
        pairs.append((ref, weight.at[pl.ds(pl.multiple_of(part * half, half), half)]))
    for copy in run_copies(pairs, sems):
        copy.wait()
    width = out_ref.shape[1] // 2
    for i in range(2):
        at = slice(i * width, (i + 1) * width)
        out_ref[:, at] = jnp.dot(grads[...], weight[:, at], preferred_element_type=F32).astype(BF16)


def back_product(line, grads, near, far):
    depth, width = grads.shape[1], far.shape[1]
    anywhere = pl.BlockSpec(memory_space=pl.ANY)
    return pl.pallas_call(
        back_kernel,
        out_shape=jax.ShapeDtypeStruct((grads.shape[0], width), BF16),
        in_specs=[pl.BlockSpec(memory_space=pltpu.SMEM)] + [anywhere] * 3,
        out_specs=pl.BlockSpec(memory_space=pltpu.VMEM),
        scratch_shapes=[
            pltpu.VMEM(grads.shape, BF16),
            pltpu.VMEM((depth, width), BF16),
            pltpu.SemaphoreType.DMA((3,)),
        ],
        compiler_params=pltpu.CompilerParams(vmem_limit_bytes=32 * 2**20),
        cost_estimate=LIGHT,
        name="back_rows",
    )(line, grads, near, far)


def over_ctx(shard):
    return lax.all_to_all(shard, "ctx", 0, 0, tiled=True)


def swap_halves(pair):
    return pltpu.roll(pair, HEAD_WIDTH, 1)


def tile_rows(index, size):
    return pl.ds(pl.multiple_of(index * size, size), size)


def last_tile(place, size, tokens):
    return place * tokens // size


def per_head(pair, tokens):
    even = slice(2 * pair * tokens, (2 * pair + 1) * tokens)
    odd = slice((2 * pair + 1) * tokens, (2 * pair + 2) * tokens)
    return slice(pair * PAIR, (pair + 1) * PAIR), even, odd


def attend_kernel(place_ref, query_ref, norm_ref, kv_ref, attend_ref, low_ref, low, norm):
    tokens, width = query_ref.shape
    j, place = pl.program_id(0), place_ref[0]
    last = last_tile(place, KEY_TILE, tokens)

    @pl.when(j == 0)
    def _():
        first = lax.broadcasted_iota(jnp.int32, (tokens, PAIR), 1) < HEAD_WIDTH
        for pair in range(width // PAIR):
            columns, even, odd = per_head(pair, tokens)
            q = query_ref[:, columns].astype(F32) * (HEAD_WIDTH**-0.5)
            low[even, :] = jnp.where(first, q, 0.0).astype(BF16)
            low[odd, :] = jnp.where(first, swap_halves(q), 0.0).astype(BF16)
            norm[:, even] = norm_ref[2 * pair : 2 * pair + 1, :]
            norm[:, odd] = norm_ref[2 * pair + 1 : 2 * pair + 2, :]
        low_ref[...] = low[...]

    def tile(masked):
        kv = kv_ref[tile_rows(j, KEY_TILE), :]
        for r in range(low.shape[0] // ROW_TILE):
            at = slice(r * ROW_TILE, (r + 1) * ROW_TILE)
            scores = lax.dot_general(kv, low[at, :], NT, preferred_element_type=F32)
            attend = jnp.exp(scores - norm[:, at])
            if masked:
                key_pos = j * KEY_TILE + lax.broadcasted_iota(jnp.int32, attend.shape, 0)
                token = lax.broadcasted_iota(jnp.int32, attend.shape, 1) % tokens
                attend = jnp.where(key_pos <= place * tokens + token, attend, 0.0)
            attend_ref[:, at] = attend.astype(BF16)

    pl.when(j < last)(lambda: tile(False))
    pl.when(j == last)(lambda: tile(True))


def key_value_kernel(
    place_ref, mix_ref, rows_ref, grad_out_ref, out_ref, attend_ref, low_ref, kv_ref,
    hidden_ref, sum_ref, high, delta,
):
    tokens, width = grad_out_ref.shape
    j, place = pl.program_id(0), place_ref[0]
    last = last_tile(place, KEY_TILE, tokens)

    @pl.when(j == 0)
    def _():
        first = lax.broadcasted_iota(jnp.int32, (tokens, PAIR), 1) < HEAD_WIDTH
        mixed = jnp.dot(mix_ref[...], rows_ref[...], preferred_element_type=F32)
        hidden = (
            grad_out_ref[...].astype(F32)
            + (mixed[:tokens] + (mixed[tokens : 2 * tokens] + mixed[2 * tokens :]))
        ).astype(BF16)
        hidden_ref[...] = hidden
        for pair in range(width // PAIR):
            columns, even, odd = per_head(pair, tokens)
            g = hidden[:, columns].astype(F32)
            high[even, :] = jnp.where(first, 0.0, swap_halves(g)).astype(BF16)
            high[odd, :] = jnp.where(first, 0.0, g).astype(BF16)
            prod = (g * out_ref[:, columns].astype(F32)).T
            delta[:, even] = jnp.sum(prod[:HEAD_WIDTH], axis=0, keepdims=True)
            delta[:, odd] = jnp.sum(prod[HEAD_WIDTH:], axis=0, keepdims=True)

    @pl.when(j <= last)
    def _():
        kv = kv_ref[tile_rows(j, KEY_TILE), :]
        total = jnp.zeros((KEY_TILE, PAIR), F32)
        for r in range(high.shape[0] // ROW_TILE):
            at = slice(r * ROW_TILE, (r + 1) * ROW_TILE)
            g = high[at, :]
            attend = attend_ref[:, at]
            prob = lax.dot_general(kv, g, NT, preferred_element_type=F32)
            score_grad = (attend.astype(F32) * (prob - delta[:, at])).astype(BF16)
            total = total + jnp.dot(score_grad, low_ref[at, :], preferred_element_type=F32)
            total = total + jnp.dot(attend, g, preferred_element_type=F32)
        sum_ref[...] = total.astype(BF16)

    @pl.when(j > last)
    def _():
        sum_ref[...] = jnp.zeros_like(sum_ref)


def query_kernel(
    place_ref, hidden_ref, out_ref, low_ref, norm_ref, kv_ref, grad_ref, high, norm, delta, total
):
    tokens, width = hidden_ref.shape
    j, place = pl.program_id(0), place_ref[0]
    last = last_tile(place, QUERY_KEY_TILE, tokens)
    first = lax.broadcasted_iota(jnp.int32, (tokens, PAIR), 1) < HEAD_WIDTH

    @pl.when(j == 0)
    def _():
        norms = norm_ref[...].T
        for pair in range(width // PAIR):
            columns, even, odd = per_head(pair, tokens)
            g = hidden_ref[:, columns].astype(F32)
            high[even, :] = jnp.where(first, 0.0, swap_halves(g)).astype(BF16)
            high[odd, :] = jnp.where(first, 0.0, g).astype(BF16)
            prod = g * out_ref[:, columns].astype(F32)
            delta[even, :] = jnp.sum(jnp.where(first, prod, 0.0), axis=1, keepdims=True)
            delta[odd, :] = jnp.sum(jnp.where(first, 0.0, prod), axis=1, keepdims=True)
            norm[even, :] = norms[:, 2 * pair : 2 * pair + 1]
            norm[odd, :] = norms[:, 2 * pair + 1 : 2 * pair + 2]
        total[...] = jnp.zeros_like(total)

    def tile(masked):
        kv = kv_ref[tile_rows(j, QUERY_KEY_TILE), :]
        for r in range(high.shape[0] // QUERY_ROW_TILE):
            at = slice(r * QUERY_ROW_TILE, (r + 1) * QUERY_ROW_TILE)
            scores = lax.dot_general(low_ref[at, :], kv, NT, preferred_element_type=F32)
            attend = jnp.exp(scores - norm[at, :])
            if masked:
                key_pos = j * QUERY_KEY_TILE + lax.broadcasted_iota(jnp.int32, attend.shape, 1)
                token = lax.broadcasted_iota(jnp.int32, attend.shape, 0) % tokens
                attend = jnp.where(key_pos <= place * tokens + token, attend, 0.0)
            prob = lax.dot_general(high[at, :], kv, NT, preferred_element_type=F32)
            score_grad = (attend * (prob - delta[at, :])).astype(BF16)
            total[at, :] += jnp.dot(score_grad, kv, preferred_element_type=F32)

    pl.when(j < last)(lambda: tile(False))
    pl.when(j == last)(lambda: tile(True))

    @pl.when(j == pl.num_programs(0) - 1)
    def _():
        for pair in range(width // PAIR):
            columns, even, odd = per_head(pair, tokens)
            both = jnp.where(first, total[even, :], swap_halves(total[odd, :]))
            grad_ref[:, columns] = (both * (HEAD_WIDTH**-0.5)).astype(BF16)


def whole(array):
    return pl.BlockSpec(array.shape, lambda j, place: (0, 0))


def call(kernel, name, steps, in_specs, out_specs, out_shape, scratch, matmuls, elements, place, *operands):
    return pl.pallas_call(
        kernel,
        out_shape=out_shape,
        grid_spec=pltpu.PrefetchScalarGridSpec(
            num_scalar_prefetch=1,
            grid=(steps,),
            in_specs=in_specs,
            out_specs=out_specs,
            scratch_shapes=scratch,
        ),
        compiler_params=pltpu.CompilerParams(vmem_limit_bytes=60 * 2**20),
        cost_estimate=LIGHT,
        name=name,
    )(place, *operands)


def attend_block(tokens):
    return lambda j, place: (jnp.minimum(j, last_tile(place[0], KEY_TILE, tokens)), 0)


def attention_weights(place, queries, norms, kv):
    tokens, width = queries.shape
    keys, rows = kv.shape[0], width // HEAD_WIDTH * tokens
    out = (jax.ShapeDtypeStruct((keys, rows), BF16), jax.ShapeDtypeStruct((rows, PAIR), BF16))
    return call(
        attend_kernel,
        "attend",
        keys // KEY_TILE,
        [whole(queries), whole(norms), whole(kv)],
        (pl.BlockSpec((KEY_TILE, rows), attend_block(tokens)), whole(out[1])),
        out,
        [pltpu.VMEM((rows, PAIR), BF16), pltpu.VMEM((1, rows), F32)],
        1,
        keys * rows,
        place,
        queries,
        norms,
        kv,
    )


def key_value_grads(place, mix, rows, grad_out, attn_out, attend, low, kv):
    tokens, width = grad_out.shape
    keys, lines = attend.shape
    out = (jax.ShapeDtypeStruct((tokens, width), BF16), jax.ShapeDtypeStruct((keys, PAIR), BF16))
    return call(
        key_value_kernel,
        "key_value_grads",
        keys // KEY_TILE,
        [whole(mix), whole(rows), whole(grad_out), whole(attn_out)]
        + [pl.BlockSpec((KEY_TILE, lines), attend_block(tokens)), whole(low), whole(kv)],
        (whole(out[0]), pl.BlockSpec((KEY_TILE, PAIR), lambda j, place: (j, 0))),
        out,
        [pltpu.VMEM((lines, PAIR), BF16), pltpu.VMEM((1, lines), F32)],
        3,
        keys * lines,
        place,
        mix,
        rows,
        grad_out,
        attn_out,
        attend,
        low,
        kv,
    )


def query_grads(place, hidden, attn_out, low, norms, kv):
    keys, lines = kv.shape[0], low.shape[0]
    out = jax.ShapeDtypeStruct(hidden.shape, BF16)
    return call(
        query_kernel,
        "query_grads",
        keys // QUERY_KEY_TILE,
        [whole(x) for x in (hidden, attn_out, low, norms, kv)],
        whole(out),
        out,
        [
            pltpu.VMEM((lines, PAIR), BF16),
            pltpu.VMEM((lines, 1), F32),
            pltpu.VMEM((lines, 1), F32),
            pltpu.VMEM((lines, PAIR), F32),
        ],
        3,
        keys * lines,
        place,
        hidden,
        attn_out,
        low,
        norms,
        kv,
    )


def as_one(steps, step, *shapes):
    init = tuple(jnp.zeros(shape, BF16) for shape in shapes)
    return lax.fori_loop(0, steps, lambda i, carry: step(i.astype(jnp.int32)), init)


def pack_kernel(step_ref, key_ref, value_ref, kv_ref):
    del step_ref
    tokens = key_ref.shape[1]
    keys, values = key_ref[...].astype(F32).T.astype(BF16), value_ref[...].astype(F32).T.astype(BF16)
    for i in range(kv_ref.shape[0] // tokens):
        kv_ref[i * tokens : (i + 1) * tokens, :HEAD_WIDTH] = keys
        kv_ref[i * tokens : (i + 1) * tokens, HEAD_WIDTH:] = values


def over_chips(step, keys, values):
    chips = lax.axis_size("ctx") // 2
    vmem = pl.BlockSpec(memory_space=pltpu.VMEM)
    copies = pl.pallas_call(
        pack_kernel,
        out_shape=jax.ShapeDtypeStruct((chips * keys.shape[0], PAIR), BF16),
        in_specs=[pl.BlockSpec(memory_space=pltpu.SMEM)] + [vmem] * 2,
        out_specs=vmem,
        cost_estimate=LIGHT,
        name="pack",
    )(step.reshape(1), keys.T, values.T)
    same_core = [[2 * i + core for i in range(chips)] for core in range(2)]
    return lax.all_to_all(copies, "ctx", 0, 0, tiled=True, axis_index_groups=same_core)


def with_other_core(mine):
    devices = lax.axis_size("ctx")
    theirs = lax.ppermute(mine, "ctx", [(i, i ^ 1) for i in range(devices)])
    first = lax.axis_index("ctx") % 2 == 0
    parts = [x.reshape(devices // 2, -1, PAIR) for x in (mine, theirs)]
    both = jnp.stack([jnp.where(first, parts[0], parts[1]), jnp.where(first, parts[1], parts[0])], axis=1)
    return both.reshape(2 * mine.shape[0], PAIR)


def sum_kernel(parts_ref, key_ref, value_ref):
    total = jnp.sum(parts_ref[...].astype(F32), axis=0).T
    key_ref[...] = total[:HEAD_WIDTH].astype(BF16)
    value_ref[...] = total[HEAD_WIDTH:].astype(BF16)


def sum_parts(parts):
    vmem = pl.BlockSpec(memory_space=pltpu.VMEM)
    out = jax.ShapeDtypeStruct((HEAD_WIDTH, parts.shape[1]), BF16)
    keys, values = pl.pallas_call(
        sum_kernel,
        out_shape=(out, out),
        in_specs=[vmem],
        out_specs=(vmem, vmem),
        cost_estimate=LIGHT,
        name="sum_parts",
    )(parts)
    return keys.T, values.T


def mix_matrix(routes, gates, experts, capacity):
    tokens, top = routes.shape
    flat = routes.reshape(-1)
    number = jnp.arange(flat.shape[0], dtype=jnp.int32)
    same = (flat[:, None] == flat[None, :]) & (number[None, :] < number[:, None])
    slots = (flat * capacity + jnp.sum(same.astype(jnp.int32), axis=1)).reshape(tokens, top)
    terms, left = [], gates
    for _ in range(3):
        term = left.astype(BF16)
        left = left - term.astype(F32)
        terms.append(term)
    columns = jnp.arange(experts * capacity, dtype=jnp.int32)
    hit = slots[:, :, None] == columns[None, None, :]
    return jnp.concatenate(
        [sum(jnp.where(hit[:, k], t[:, k, None], 0).astype(BF16) for k in range(top)) for t in terms], axis=0
    )


def body(
    queries,
    saved_key_rows,
    saved_value_rows,
    attn_out,
    log_sum_norm,
    grad_out,
    routes,
    gates,
    expert_in,
    hidden_grad,
    up_weight,
):
    experts = lax.axis_size("ctx")
    place = lax.axis_index("ctx").astype(jnp.int32).reshape(1)
    line = lax.axis_index("dp")
    x, y = line % X_RING, line // X_RING
    tokens, width = queries.shape
    capacity = hidden_grad.shape[2] // experts
    weight = up_weight[0]
    shard_rows = weight.shape[0]
    half_rows = X_RING * shard_rows

    steps = 1 - place[0] // experts
    keys, pairs = experts * tokens, width // HEAD_WIDTH * tokens

    crossed = other_y(weight)
    near = lax.all_gather(weight, "dp", axis=0, tiled=True, axis_index_groups=X_GROUPS)

    chips = experts // 2
    (kv,) = as_one(
        steps, lambda i: (over_chips(i, saved_key_rows, saved_value_rows),), (chips * tokens, PAIR)
    )
    crossed, kv, routes = lax.optimization_barrier((crossed, kv, routes))
    kv = with_other_core(kv)
    copies = repeated(crossed)
    copies, slot_grads, inputs = lax.optimization_barrier((copies, hidden_grad[0, 0], expert_in[0, 0]))
    far = over_x(copies)

    def weight_term(half):
        grads = lax.dynamic_slice_in_dim(slot_grads, half * half_rows, half_rows, 1)
        return lax.dot_general(grads, inputs, TN, preferred_element_type=F32).astype(BF16)

    def x_sum(term):
        return lax.psum_scatter(term, "dp", scatter_dimension=0, tiled=True, axis_index_groups=X_GROUPS)

    attend, low = attention_weights(place, queries, log_sum_norm, kv)
    far, attend, low, term_far, term_near = lax.optimization_barrier(
        (far, attend, low, weight_term(1 - y), weight_term(y))
    )
    sum_far = x_sum(term_far)
    sum_near = x_sum(term_near)
    rows = over_ctx(back_product(line.astype(jnp.int32).reshape(1), slot_grads, near, far))
    mix = mix_matrix(routes, gates, experts, capacity)

    sum_far = other_y(sum_far)

    def attention(i):
        grad_hidden, total = key_value_grads(place + i, mix, rows, grad_out, attn_out, attend, low, kv)
        parts = over_ctx(total)
        query_gradient = query_grads(place + i, grad_hidden, attn_out, low, log_sum_norm, kv)
        return grad_hidden, query_gradient, parts

    grad_hidden, query_gradient, parts = as_one(
        steps, attention, (tokens, width), (tokens, width), (keys, PAIR)
    )
    key_gradient, value_gradient = sum_parts(parts.reshape(experts, tokens, PAIR))
    grad_up = (sum_near.astype(F32) + sum_far.astype(F32)).astype(BF16).reshape(up_weight.shape)
    return grad_hidden, query_gradient, key_gradient, value_gradient, grad_up


def solution(mesh):
    placed = (
        P(("dp", "ctx"), "exp"),
        P(("dp", "ctx"), "exp"),
        P(("dp", "ctx"), "exp"),
        P(("dp", "ctx"), "exp"),
        P("exp", ("dp", "ctx")),
        P(("dp", "ctx"), "exp"),
        P(("dp", "ctx"), None),
        P(("dp", "ctx"), None),
        P("dp", "ctx", None, "exp"),
        P("dp", "ctx", None, None),
        P("ctx", "dp", "exp"),
    )
    return jax.shard_map(
        body,
        mesh=mesh,
        in_specs=placed,
        out_specs=(
            P(("dp", "ctx"), "exp"),
            P(("dp", "ctx"), "exp"),
            P(("dp", "ctx"), "exp"),
            P(("dp", "ctx"), "exp"),
            P("ctx", "dp", "exp"),
        ),
        check_vma=False,
    )
```

time: 264 us -> 153 us (0.58); the launches traced: 259 us -> 152 us
  waiting for transfers between devices: 138 us -> 45.6 us
  starting transfers between devices: 82.7 us -> 51 us
  Pallas kernels: 0 us -> 21.8 us
  matrix products: 12.4 us -> 6.69 us
  local copies, waits for them, and re-layouts: 6.01 us -> 9.4 us
    all_gather x1, waiting for transfers between devices: 95.9 us -> 0.02 us  [body(): lax.all_gather(weight, 'dp', axis=0, tiled=True, axis_index_groups=X_GROUPS)]
    ppermute x64 -> x3, starting transfers between devices: 75.8 us -> 20.3 us  [the longest x2 15.3 us: other_y(): lax.ppermute(shard, 'dp', [(i, (i + X_RING) % (2 * X_RING)) for i in rang...]
    all_to_all x1 -> x4, starting transfers between devices: 6.82 us -> 30.7 us  [the longest x2 16.5 us: over_ctx(): return lax.all_to_all(shard, 'ctx', 0, 0, tiled=True)]
    pallas_call x0 -> x7, Pallas kernels: none -> 21.8 us  [the longest x3 14 us: call(): pl.pallas_call(kernel, out_shape=out_shape, grid_spec=pltpu.PrefetchScala...]
    ppermute x64 -> x3, waiting for transfers between devices: 16.5 us -> 0.01 us  [the longest x2 0.01 us: other_y(): lax.ppermute(shard, 'dp', [(i, (i + X_RING) % (2 * X_RING)) for i in rang...]
    reduce_scatter x1 -> x2, waiting for transfers between devices: 0.01 us -> 14.7 us  [x_sum(): lax.psum_scatter(term, 'dp', scatter_dimension=0, tiled=True, axis_index_...]
    dot_general x12 -> x2, matrix products: 12.4 us -> 6.69 us  [weight_term(): lax.dot_general(grads, inputs, TN, preferred_element_type=F32).astype(BF16)]
    all_to_all x1 -> x4, waiting for transfers between devices: 25.2 us -> 29.5 us  [the longest x2 17.3 us: over_ctx(): return lax.all_to_all(shard, 'ctx', 0, 0, tiled=True)]
  transfers between devices with their start and end apart: 67 -> 10, of which waited for: 34 -> 5; matrix products, arithmetic and copies ran while one was open for 9% -> 8% of each run, Pallas kernels for 0% -> 14%
where the time goes in v1:
time: 153 us; the launch traced here: 152 us
  starting transfers between devices  51 us (33%)
  waiting for transfers between devices  45.6 us (30%)
  Pallas kernels  21.8 us (14%)
  between operations  13.9 us (9%)
  local copies, waits for them, and re-layouts  9.4 us (6%)
  matrix products  6.69 us (4%)
  other arithmetic  3.37 us (2%)
    all_to_all x2, waiting for transfers between devices, over_ctx(): return lax.all_to_all(shard, 'ctx', 0, 0, tiled=True)  17.3 us
    all_to_all x2, starting transfers between devices, over_ctx(): return lax.all_to_all(shard, 'ctx', 0, 0, tiled=True)  16.5 us
    ppermute x2, starting transfers between devices, other_y(): lax.ppermute(shard, 'dp', [(i, (i + X_RING) % (2 * X_RING)) for i in rang...  15.3 us
    reduce_scatter x2, waiting for transfers between devices, x_sum(): lax.psum_scatter(term, 'dp', scatter_dimension=0, tiled=True, axis_index_...  14.7 us
    pallas_call x3, Pallas kernels, call(): pl.pallas_call(kernel, out_shape=out_shape, grid_spec=pltpu.PrefetchScala...  14 us
    all_to_all x1, waiting for transfers between devices, over_chips(): lax.all_to_all(copies, 'ctx', 0, 0, tiled=True, axis_index_groups=same_core)  10.1 us
    all_to_all x1, starting transfers between devices, over_chips(): lax.all_to_all(copies, 'ctx', 0, 0, tiled=True, axis_index_groups=same_core)  10 us
    dot_general x2, matrix products, weight_term(): lax.dot_general(grads, inputs, TN, preferred_element_type=F32).astype(BF16)  6.69 us
  transfers between devices with their start and end apart: 10, of which 5 were waited for; matrix products, arithmetic and copies ran while one was open for 8% of the time, Pallas kernels for 14%

profile of v1, /device:TPU:1, one launch (start us, length us, event | category | flops | bytes accessed | tf_op | source)
XLA Modules:
  0.0 151.8 jit_solution(1563900092774723511)
XLA Ops:
  7.2 0.0 all-gather.3.cloned.1.call-start
  7.2 0.7 all-gather.3.cloned.1.call-update
  7.9 8.3 %collective-permute-start = (bf16[192,1024]{1,0:T(8,128)(2,1)}, bf16[192,1024]{1,0:T(8,128)(2,1)S(1)}, u32[]{:S(2)}, u32[]{:S(2)}) collective-permute-start(bf16[192,1024]{1,0:T(8,128)(2,1)} %bitcast.107), channel_id=1, source_target_pairs={{0,256},{64,320},{128,384},{192,448},{256,0},{320,64},{384,128},{4... | collective-permute-start | bytes 1179656 | tf_op jit(solution)/shard_map/ppermute | solution.py:27
  16.2 0.7 broadcast_in_dim.64
  17.0 22.4 %while.24 = (s32[]{:T(128)}, bf16[1024,128]{1,0:T(8,128)(2,1)}, s32[]{:T(128)}, bf16[128,64]{0,1:T(8,128)(2,1)}, bf16[128,64]{0,1:T(8,128)(2,1)}, /*index=5*/s32[]{:T(128)}) while((s32[]{:T(128)}, bf16[1024,128]{1,0:T(8,128)(2,1)}, s32[]{:T(128)}, bf16[128,64]{0,1:T(8,128)(2,1)}, bf16[128,64]{0,1:T(8,128)(2,1)}, /*index=5*/s32[]{:T(128)}) %tuple.51), condition=%wide.region_1.2_spmd, body=%wide.region_0.1_spmd.sunk | while | flops 1048578 | bytes 1900673 | solution.py:346
  17.0 1.6 %pack.1 = bf16[1024,128]{1,0:T(8,128)(2,1)} custom-call(s32[1]{0:T(128)} %bitcast.80.step_ref, bf16[64,128]{1,0:T(8,128)(2,1)} %bitcast.105, bf16[64,128]{1,0:T(8,128)(2,1)} %bitcast.106), custom_call_target="tpu_custom_call" | custom-call | flops 1048576 | bytes 65536 | tf_op jit(solution)/shard_map/while/body/pack/pallas_call | solution.py:361
  18.6 10.0 %all-to-all-start = ((bf16[8,128,128]{2,1,0:T(8,128)(2,1)}), bf16[8,128,128]{2,1,0:T(8,128)(2,1)S(1)}, u32[]{:S(2)}, u32[]{:S(2)}) async-start(bf16[8,128,128]{2,1,0:T(8,128)(2,1)} %bitcast.99), calls=%async_computation | async-start | bytes 524288 | tf_op jit(solution)/shard_map/while/body/all_to_all | solution.py:370
  28.6 10.1 %all-to-all-done = bf16[8,128,128]{2,1,0:T(8,128)(2,1)S(1)} async-done(((bf16[8,128,128]{2,1,0:T(8,128)(2,1)}), bf16[8,128,128]{2,1,0:T(8,128)(2,1)S(1)}, u32[]{:S(2)}, u32[]{:S(2)}) %all-to-all-start) | async-done | bytes 262176 | tf_op jit(solution)/shard_map/while/body/all_to_all | solution.py:370
  38.7 0.7 copy-done.6
  39.4 0.7 copy-done.8
  40.1 2.3 %repeat.1 = bf16[768,1024]{1,0:T(8,128)(2,1)} custom-call(bf16[192,1024]{1,0:T(8,128)(2,1)} %copy-done.8), custom_call_target="tpu_custom_call" | custom-call | flops 1048576 | bytes 65536 | tf_op jit(solution)/shard_map/repeat/pallas_call | solution.py:50
  42.4 4.1 %all-to-all-start.2 = ((bf16[4,192,1024]{2,1,0:T(8,128)(2,1)}), bf16[4,192,1024]{2,1,0:T(8,128)(2,1)S(1)}, u32[]{:S(2)}, u32[]{:S(2)}) async-start(bf16[4,192,1024]{2,1,0:T(8,128)(2,1)} %bitcast.101), calls=%async_computation.2 | async-start | bytes 3145728 | tf_op jit(solution)/shard_map/all_to_all | solution.py:61
  46.6 4.9 %collective-permute-start.1 = (bf16[1024,128]{1,0:T(8,128)(2,1)S(1)}, bf16[1024,128]{1,0:T(8,128)(2,1)S(1)}, u32[]{:S(2)}, u32[]{:S(2)}) collective-permute-start(bf16[1024,128]{1,0:T(8,128)(2,1)S(1)} %copy-done.7), channel_id=1, source_target_pairs={{0,4},{4,0},{8,12},{12,8},{16,20},{20,16},{24,28},{28,24},{32,36},... | collective-permute-start | bytes 786440 | tf_op jit(solution)/shard_map/ppermute | solution.py:375
  51.5 3.4 %convolution_convert_fusion.1 = bf16[768,1024]{1,0:T(8,128)(2,1)} fusion(bf16[512,1024]{1,0:T(8,128)(2,1)S(1)} %bitcast.89, bf16[512,1536]{1,0:T(8,128)(2,1)} %bitcast.92, s32[]{:T(128)S(6)} %select_n.85), kind=kOutput, calls=%fused_computation.1 | convolution fusion | flops 806092800 | bytes 3407876 | tf_op jit(solution)/shard_map/dot_general | solution.py:461
  54.9 3.3 %convolution_convert_fusion = bf16[768,1024]{1,0:T(8,128)(2,1)} fusion(bf16[512,1024]{1,0:T(8,128)(2,1)S(1)} %bitcast.88, bf16[512,1536]{1,0:T(8,128)(2,1)} %bitcast.93, s32[]{:T(128)S(6)} %select_n.86), kind=kOutput, calls=%fused_computation | convolution fusion | flops 806092800 | bytes 3407876 | tf_op jit(solution)/shard_map/dot_general | solution.py:461
  58.2 0.1 pad_maximum_fusion
  58.3 0.6 copy-done.9
  58.9 3.3 %attend.1 = (bf16[2048,2048]{1,0:T(8,128)(2,1)}, bf16[2048,128]{1,0:T(8,128)(2,1)}) custom-call(s32[1]{0:T(128)} %bitcast.8.place_ref, bf16[128,1024]{1,0:T(8,128)(2,1)} %query_ref.1, f32[16,128]{1,0:T(8,128)S(1)} %copy-done.9, bf16[2048,128]{1,0:T(8,128)(2,1)S(1)} %bitcast.96), custom_call_target="tpu_custom_call" | custom-call | flops 1048576 | bytes 65536 | tf_op jit(solution)/shard_map/attend/pallas_call | solution.py:250
  62.1 2.1 %all-to-all-done.2 = bf16[4,192,1024]{2,1,0:T(8,128)(2,1)S(1)} async-done(((bf16[4,192,1024]{2,1,0:T(8,128)(2,1)}), bf16[4,192,1024]{2,1,0:T(8,128)(2,1)S(1)}, u32[]{:S(2)}, u32[]{:S(2)}) %all-to-all-start.2) | async-done | bytes 1572896 | tf_op jit(solution)/shard_map/all_to_all | solution.py:61
  64.3 0.0 reduce-scatter.3.cloned.1.call-start
  64.3 0.7 reduce-scatter.3.cloned.1.call-update
  65.0 0.0 all-gather.3.cloned.1.call-done
  65.1 1.4 copy-done.2
  66.5 1.4 copy-done.3
  67.9 2.1 %back_rows.1 = bf16[512,1024]{1,0:T(8,128)(2,1)S(1)} custom-call(s32[1]{0:T(128)} %bitcast.18.line_ref, bf16[512,1536]{1,0:T(8,128)(2,1)S(1)} %bitcast.94, bf16[768,1024]{1,0:T(8,128)(2,1)S(1)} %bitcast.95, bf16[768,1024]{1,0:T(8,128)(2,1)S(1)} %bitcast.90), custom_call_target="tpu_custom_call" | custom-call | flops 1048576 | bytes 65536 | tf_op jit(solution)/shard_map/back_rows/pallas_call | solution.py:81
  70.0 1.0 copy-done.1
  71.0 8.1 %all-to-all-start.3 = ((bf16[16,32,1024]{2,1,0:T(8,128)(2,1)}), bf16[16,32,1024]{2,1,0:T(8,128)(2,1)S(1)}, u32[]{:S(2)}, u32[]{:S(2)}) async-start(bf16[16,32,1024]{2,1,0:T(8,128)(2,1)} %bitcast.91), calls=%async_computation.3 | async-start | bytes 2097152 | tf_op jit(solution)/shard_map/all_to_all | solution.py:98
  79.2 0.1 copy.30
  79.3 0.1 eq.33
  79.5 0.2 convert_reduce_fusion
  79.7 0.1 reduce_sum.12
  79.8 0.1 copy.31
  79.9 14.7 %reduce-scatter.5.cloned.1.call-done = bf16[192,1024]{1,0:T(8,128)(2,1)} async-done(((bf16[768,1024]{1,0:T(8,128)(2,1)}), bf16[192,1024]{1,0:T(8,128)(2,1)}) %reduce-scatter.5.cloned.1.call-update) | async-done | bytes 393232 | tf_op jit(solution)/shard_map/reduce_scatter | solution.py:464
  94.6 7.1 %collective-permute-start.2 = (bf16[192,1024]{1,0:T(8,128)(2,1)}, bf16[192,1024]{1,0:T(8,128)(2,1)}, u32[]{:S(2)}, u32[]{:S(2)}) collective-permute-start(bf16[192,1024]{1,0:T(8,128)(2,1)} %reduce-scatter.5.cloned.1.call-done), channel_id=1, source_target_pairs={{0,256},{64,320},{128,384},{192,448},{256,0},{320,64},{384,128},{4... | collective-permute-start | bytes 1179656 | tf_op jit(solution)/shard_map/ppermute | solution.py:27
  101.7 0.1 iota_compare_fusion
  101.8 0.2 fusion.10
  102.0 0.8 pad_maximum_fusion.1
  102.8 4.7 %all-to-all-done.3 = bf16[16,32,1024]{2,1,0:T(8,128)(2,1)S(1)} async-done(((bf16[16,32,1024]{2,1,0:T(8,128)(2,1)}), bf16[16,32,1024]{2,1,0:T(8,128)(2,1)S(1)}, u32[]{:S(2)}, u32[]{:S(2)}) %all-to-all-start.3) | async-done | bytes 1048608 | tf_op jit(solution)/shard_map/all_to_all | solution.py:98
  107.5 0.9 broadcast_in_dim.63
  108.4 0.7 broadcast.26
  109.1 0.7 broadcast.26.clone
  109.8 31.6 %while.25 = (s32[]{:T(128)}, bf16[128,1024]{1,0:T(8,128)(2,1)}, bf16[128,1024]{1,0:T(8,128)(2,1)}, bf16[2048,128]{1,0:T(8,128)(2,1)}, s32[]{:T(128)}, /*index=5*...) while((s32[]{:T(128)}, bf16[128,1024]{1,0:T(8,128)(2,1)}, ...), condition=%wide.region_4.5_spmd, body=%wide.region_3.4_spmd.sunk | while | flops 2097155 | bytes 1704121 | solution.py:346
  109.8 5.9 %key_value_grads.1 = (bf16[128,1024]{1,0:T(8,128)(2,1)}, bf16[2048,128]{1,0:T(8,128)(2,1)}) custom-call(s32[1]{0:T(128)S(6)} %add.67.place_ref, bf16[384,512]{1,0:T(8,128)(2,1)} %get-tuple-element.362.mix_ref, bf16[512,1024]{1,0:T(8,128)(2,1)S(1)} %get-tuple-element.363.rows_ref, bf16[128,1024]{1,0:T(8,128)(2,1)} %get-tuple-element.364.grad_out_ref, ...), custom_call_target="tpu_custom_call" | custom-call | flops 1048576 | bytes 65536 | tf_op jit(solution)/shard_map/while/body/key_value_grads/pallas_call | solution.py:250
  115.7 8.3 %all-to-all-start.1 = ((bf16[16,128,128]{2,1,0:T(8,128)(2,1)}), bf16[16,128,128]{2,1,0:T(8,128)(2,1)}, u32[]{:S(2)}, u32[]{:S(2)}) async-start(bf16[16,128,128]{2,1,0:T(8,128)(2,1)} %bitcast.100), calls=%async_computation.1 | async-start | bytes 1048576 | tf_op jit(solution)/shard_map/while/body/all_to_all | solution.py:98
  124.0 4.9 %query_grads.1 = bf16[128,1024]{1,0:T(8,128)(2,1)} custom-call(s32[1]{0:T(128)S(6)} %add.67.place_ref, bf16[128,1024]{1,0:T(8,128)(2,1)} %get-tuple-element.357.hidden_ref, bf16[128,1024]{1,0:T(8,128)(2,1)S(1)} %get-tuple-element.365.out_ref, bf16[2048,128]{1,0:T(8,128)(2,1)S(1)} %get-tuple-element.367.low_ref, f32[16,128]{1,0:T(8,128)S(1)} %get-tuple-element.369.norm_ref, ...), custom_call_target="tpu_custom_call" | custom-call | flops 1048576 | bytes 65536 | tf_op jit(solution)/shard_map/while/body/query_grads/pallas_call | solution.py:250
  128.9 12.6 %all-to-all-done.1 = bf16[16,128,128]{2,1,0:T(8,128)(2,1)} async-done(((bf16[16,128,128]{2,1,0:T(8,128)(2,1)}), bf16[16,128,128]{2,1,0:T(8,128)(2,1)}, u32[]{:S(2)}, u32[]{:S(2)}) %all-to-all-start.1) | async-done | bytes 524320 | tf_op jit(solution)/shard_map/while/body/all_to_all | solution.py:98
  141.5 1.8 %sum_parts.1 = (bf16[64,128]{1,0:T(8,128)(2,1)}, bf16[64,128]{1,0:T(8,128)(2,1)}) custom-call(bf16[16,128,128]{2,1,0:T(8,128)(2,1)} %bitcast.31.parts_ref), custom_call_target="tpu_custom_call" | custom-call | flops 1048576 | bytes 65536 | tf_op jit(solution)/shard_map/sum_parts/pallas_call | solution.py:391
  143.3 2.0 %fusion.2 = bf16[1,192,1024]{2,1,0:T(8,128)(2,1)} fusion(bf16[192,1024]{1,0:T(8,128)(2,1)} %collective-permute-done.2, bf16[192,1024]{1,0:T(8,128)(2,1)} %reduce-scatter.3.cloned.1.call-done), kind=kLoop, calls=%fused_computation.7 | loop fusion | flops 786432 | bytes 1179648 | tf_op jit(solution)/shard_map/reshape | solution.py:487
  (29 shorter events, 0.1 us)
Async XLA Ops:
  7.2 35.2 %copy-start = (bf16[1,1,512,1024]{3,2,1,0:T(8,128)(2,1)S(1)}, bf16[1,1,512,1024]{3,2,1,0:T(8,128)(2,1)}, u32[]{:S(2)}) copy-start(bf16[1,1,512,1024]{3,2,1,0:T(8,128)(2,1)} %param.23) | copy-start | bytes 3145732
  7.2 57.9 %all-gather.3.cloned.1.call-start = ((), (), s32[]{:S(2)}) async-start(), calls=%async_computation.8 | async-start | bytes 1966080 | tf_op jit(solution)/shard_map/all_gather | solution.py:447
  7.9 31.5 %collective-permute-start = (bf16[192,1024]{1,0:T(8,128)(2,1)}, bf16[192,1024]{1,0:T(8,128)(2,1)S(1)}, u32[]{:S(2)}, u32[]{:S(2)}) collective-permute-start(bf16[192,1024]{1,0:T(8,128)(2,1)} %bitcast.107), channel_id=1, source_target_pairs={{0,256},{64,320},{128,384},{192,448},{256,0},{320,64},{384,128},{4... | collective-permute-start | bytes 1179656 | tf_op jit(solution)/shard_map/ppermute | solution.py:27
  18.6 20.1 %all-to-all-start = ((bf16[8,128,128]{2,1,0:T(8,128)(2,1)}), bf16[8,128,128]{2,1,0:T(8,128)(2,1)S(1)}, u32[]{:S(2)}, u32[]{:S(2)}) async-start(bf16[8,128,128]{2,1,0:T(8,128)(2,1)} %bitcast.99), calls=%async_computation | async-start | bytes 524288 | tf_op jit(solution)/shard_map/while/body/all_to_all | solution.py:370
  38.7 0.7 copy-start.6
  39.4 0.7 copy-start.8
  42.4 4.1 %copy-start.7 = (bf16[1024,128]{1,0:T(8,128)(2,1)S(1)}, bf16[1024,128]{1,0:T(8,128)(2,1)}, u32[]{:S(2)}) copy-start(bf16[1024,128]{1,0:T(8,128)(2,1)} %get-tuple-element.126) | copy-start | bytes 786436
  42.4 21.9 %all-to-all-start.2 = ((bf16[4,192,1024]{2,1,0:T(8,128)(2,1)}), bf16[4,192,1024]{2,1,0:T(8,128)(2,1)S(1)}, u32[]{:S(2)}, u32[]{:S(2)}) async-start(bf16[4,192,1024]{2,1,0:T(8,128)(2,1)} %bitcast.101), calls=%async_computation.2 | async-start | bytes 3145728 | tf_op jit(solution)/shard_map/all_to_all | solution.py:61
  46.6 48.1 %reduce-scatter.5.cloned.1.call-start = ((), (), s32[]{:S(2)}) async-start(), calls=%async_computation.7 | async-start | bytes 1966080 | tf_op jit(solution)/shard_map/reduce_scatter | solution.py:464
  46.6 11.6 %collective-permute-start.1 = (bf16[1024,128]{1,0:T(8,128)(2,1)S(1)}, bf16[1024,128]{1,0:T(8,128)(2,1)S(1)}, u32[]{:S(2)}, u32[]{:S(2)}) collective-permute-start(bf16[1024,128]{1,0:T(8,128)(2,1)S(1)} %copy-done.7), channel_id=1, source_target_pairs={{0,4},{4,0},{8,12},{12,8},{16,20},{20,16},{24,28},{28,24},{32,36},... | collective-permute-start | bytes 786440 | tf_op jit(solution)/shard_map/ppermute | solution.py:375
  58.2 0.7 copy-start.9
  64.3 79.0 %reduce-scatter.3.cloned.1.call-start = ((), (), s32[]{:S(2)}) async-start(), calls=%async_computation.6 | async-start | bytes 1966080 | tf_op jit(solution)/shard_map/reduce_scatter | solution.py:464
  65.1 1.4 copy-start.2
  66.5 1.4 copy-start.3
  70.0 1.0 copy-start.1
  71.0 8.2 %copy-start.11 = (f32[128,2]{0,1:T(2,128)S(1)}, f32[128,2]{0,1:T(2,128)}, u32[]{:S(2)}) copy-start(f32[128,2]{0,1:T(2,128)} %param.22) | copy-start | bytes 3076
  71.0 8.2 %copy-start.10 = (s32[128,2]{0,1:T(2,128)S(1)}, s32[128,2]{0,1:T(2,128)}, u32[]{:S(2)}) copy-start(s32[128,2]{0,1:T(2,128)} %param.21) | copy-start | bytes 3076
  71.0 36.5 %all-to-all-start.3 = ((bf16[16,32,1024]{2,1,0:T(8,128)(2,1)}), bf16[16,32,1024]{2,1,0:T(8,128)(2,1)S(1)}, u32[]{:S(2)}, u32[]{:S(2)}) async-start(bf16[16,32,1024]{2,1,0:T(8,128)(2,1)} %bitcast.91), calls=%async_computation.3 | async-start | bytes 2097152 | tf_op jit(solution)/shard_map/all_to_all | solution.py:98
  79.2 30.7 %copy-start.4 = (bf16[2048,128]{1,0:T(8,128)(2,1)S(1)}, bf16[2048,128]{1,0:T(8,128)(2,1)}, u32[]{:S(2)}) copy-start(bf16[2048,128]{1,0:T(8,128)(2,1)} %get-tuple-element.337) | copy-start | bytes 1572868
  79.2 30.7 %copy-start.5 = (bf16[128,1024]{1,0:T(8,128)(2,1)S(1)}, bf16[128,1024]{1,0:T(8,128)(2,1)}, u32[]{:S(2)}) copy-start(bf16[128,1024]{1,0:T(8,128)(2,1)} %param.18) | copy-start | bytes 786436
  94.6 48.6 %collective-permute-start.2 = (bf16[192,1024]{1,0:T(8,128)(2,1)}, bf16[192,1024]{1,0:T(8,128)(2,1)}, u32[]{:S(2)}, u32[]{:S(2)}) collective-permute-start(bf16[192,1024]{1,0:T(8,128)(2,1)} %reduce-scatter.5.cloned.1.call-done), channel_id=1, source_target_pairs={{0,256},{64,320},{128,384},{192,448},{256,0},{320,64},{384,128},{4... | collective-permute-start | bytes 1179656 | tf_op jit(solution)/shard_map/ppermute | solution.py:27
  115.7 25.8 %all-to-all-start.1 = ((bf16[16,128,128]{2,1,0:T(8,128)(2,1)}), bf16[16,128,128]{2,1,0:T(8,128)(2,1)}, u32[]{:S(2)}, u32[]{:S(2)}) async-start(bf16[16,128,128]{2,1,0:T(8,128)(2,1)} %bitcast.100), calls=%async_computation.1 | async-start | bytes 1048576 | tf_op jit(solution)/shard_map/while/body/all_to_all | solution.py:98
Sparse Core Ops, SparseCore 0:
  10.1 37.3 all-gather.2
  64.4 30.1 reduce-scatter.4
  97.5 30.5 reduce-scatter.2

commit v2 on v1

--- a/solution.py
+++ b/solution.py
@@ -27,11 +27,6 @@
     return lax.ppermute(shard, "dp", [(i, (i + X_RING) % (2 * X_RING)) for i in range(2 * X_RING)])
 
 
-def along_x(shard, by):
-    order = [(i, i // X_RING * X_RING + (i + by) % X_RING) for i in range(2 * X_RING)]
-    return lax.ppermute(shard, "dp", order)
-
-
 def run_copies(pairs, sems):
     copies = [pltpu.make_async_copy(src, dst, sems.at[i]) for i, (src, dst) in enumerate(pairs)]
     for copy in copies:
@@ -39,59 +34,56 @@
     return copies
 
 
-def repeat_kernel(shard_ref, out_ref):
-    rows = shard_ref.shape[0]
-    for i in range(X_RING):
-        out_ref[i * rows : (i + 1) * rows, :] = shard_ref[...]
-
-
-def repeated(shard):
-    vmem = pl.BlockSpec(memory_space=pltpu.VMEM)
-    return pl.pallas_call(
-        repeat_kernel,
-        out_shape=jax.ShapeDtypeStruct((X_RING * shard.shape[0], shard.shape[1]), shard.dtype),
-        in_specs=[vmem],
-        out_specs=vmem,
-        cost_estimate=LIGHT,
-        name="repeat",
-    )(shard)
-
-
-def over_x(shard):
-    return lax.all_to_all(shard, "dp", 0, 0, tiled=True, axis_index_groups=X_GROUPS)
-
-
-def back_kernel(line_ref, grads_ref, near_ref, far_ref, out_ref, grads, weight, sems):
-    y = line_ref[0] // X_RING
-    half = near_ref.shape[0]
-    pairs = [(grads_ref, grads)]
-    for ref, part in ((near_ref, y), (far_ref, 1 - y)):
-        pairs.append((ref, weight.at[pl.ds(pl.multiple_of(part * half, half), half)]))
+def along_x(shard, by):
+    order = [(i, i // X_RING * X_RING + (i + by) % X_RING) for i in range(2 * X_RING)]
+    return lax.ppermute(shard, "dp", order)
+
+
+def x_pieces(shard):
+    return [shard] + [along_x(shard, by) for by in range(1, X_RING)]
+
+
+def back_kernel(line_ref, grads_ref, near_ref, *rest):
+    far, (out_ref, grads, weight, back, sems) = rest[:X_RING], rest[X_RING:]
+    x, y = line_ref[0] % X_RING, line_ref[0] // X_RING
+    half, rows = near_ref.shape[0], far[0].shape[0]
+    near_rows = pl.ds(pl.multiple_of(y * half, half), half)
+    pairs = [(grads_ref, grads), (near_ref, weight.at[near_rows])]
+    for by, ref in enumerate(far):
+        start = (1 - y) * half + (x + X_RING - by) % X_RING * rows
+        pairs.append((ref, weight.at[pl.ds(pl.multiple_of(start, rows), rows)]))
     for copy in run_copies(pairs, sems):
         copy.wait()
-    width = out_ref.shape[1] // 2
-    for i in range(2):
+    parts = sems.shape[0] - len(pairs)
+    width = out_ref.shape[1] // parts
+    copies = []
+    for i in range(parts):
         at = slice(i * width, (i + 1) * width)
-        out_ref[:, at] = jnp.dot(grads[...], weight[:, at], preferred_element_type=F32).astype(BF16)
+        back[:, at] = jnp.dot(grads[...], weight[:, at], preferred_element_type=F32).astype(BF16)
+        copies.append(pltpu.make_async_copy(back.at[:, at], out_ref.at[:, at], sems.at[len(pairs) + i]))
+        copies[-1].start()
+    for copy in copies:
+        copy.wait()
 
 
 def back_product(line, grads, near, far):
-    depth, width = grads.shape[1], far.shape[1]
+    depth, width = grads.shape[1], near.shape[1]
     anywhere = pl.BlockSpec(memory_space=pl.ANY)
     return pl.pallas_call(
         back_kernel,
         out_shape=jax.ShapeDtypeStruct((grads.shape[0], width), BF16),
-        in_specs=[pl.BlockSpec(memory_space=pltpu.SMEM)] + [anywhere] * 3,
-        out_specs=pl.BlockSpec(memory_space=pltpu.VMEM),
+        in_specs=[pl.BlockSpec(memory_space=pltpu.SMEM)] + [anywhere] * (2 + X_RING),
+        out_specs=anywhere,
         scratch_shapes=[
             pltpu.VMEM(grads.shape, BF16),
             pltpu.VMEM((depth, width), BF16),
-            pltpu.SemaphoreType.DMA((3,)),
+            pltpu.VMEM((grads.shape[0], width), BF16),
+            pltpu.SemaphoreType.DMA((2 + X_RING + 4,)),
         ],
-        compiler_params=pltpu.CompilerParams(vmem_limit_bytes=32 * 2**20),
+        compiler_params=pltpu.CompilerParams(vmem_limit_bytes=60 * 2**20),
         cost_estimate=LIGHT,
         name="back_rows",
-    )(line, grads, near, far)
+    )(line, grads, near, *far)
 
 
 def over_ctx(shard):
@@ -341,13 +333,16 @@
     )
 
 
-def as_one(steps, step, *shapes):
-    init = tuple(jnp.zeros(shape, BF16) for shape in shapes)
-    return lax.fori_loop(0, steps, lambda i, carry: step(i.astype(jnp.int32)), init)
-
-
-def pack_kernel(step_ref, key_ref, value_ref, kv_ref):
-    del step_ref
+def as_one(always, step, *operands):
+    out = jax.eval_shape(step, *operands)
+
+    def never(*_):
+        return jax.tree.map(lambda x: jnp.zeros(x.shape, x.dtype), out)
+
+    return lax.cond(always, step, never, *operands)
+
+
+def pack_kernel(key_ref, value_ref, kv_ref):
     tokens = key_ref.shape[1]
     keys, values = key_ref[...].astype(F32).T.astype(BF16), value_ref[...].astype(F32).T.astype(BF16)
     for i in range(kv_ref.shape[0] // tokens):
@@ -355,17 +350,21 @@
         kv_ref[i * tokens : (i + 1) * tokens, HEAD_WIDTH:] = values
 
 
-def over_chips(step, keys, values):
+def packed(keys, values):
     chips = lax.axis_size("ctx") // 2
     vmem = pl.BlockSpec(memory_space=pltpu.VMEM)
-    copies = pl.pallas_call(
+    return pl.pallas_call(
         pack_kernel,
         out_shape=jax.ShapeDtypeStruct((chips * keys.shape[0], PAIR), BF16),
-        in_specs=[pl.BlockSpec(memory_space=pltpu.SMEM)] + [vmem] * 2,
+        in_specs=[vmem] * 2,
         out_specs=vmem,
         cost_estimate=LIGHT,
         name="pack",
-    )(step.reshape(1), keys.T, values.T)
+    )(keys.T, values.T)
+
+
+def over_chips(copies):
+    chips = lax.axis_size("ctx") // 2
     same_core = [[2 * i + core for i in range(chips)] for core in range(2)]
     return lax.all_to_all(copies, "ctx", 0, 0, tiled=True, axis_index_groups=same_core)
 
@@ -379,24 +378,26 @@
     return both.reshape(2 * mine.shape[0], PAIR)
 
 
-def sum_kernel(parts_ref, key_ref, value_ref):
+def sum_kernel(parts_ref, near_ref, far_ref, key_ref, value_ref, up_ref):
     total = jnp.sum(parts_ref[...].astype(F32), axis=0).T
     key_ref[...] = total[:HEAD_WIDTH].astype(BF16)
     value_ref[...] = total[HEAD_WIDTH:].astype(BF16)
-
-
-def sum_parts(parts):
+    up_ref[...] = (near_ref[...].astype(F32) + far_ref[...].astype(F32)).astype(BF16)
+
+
+def final_sums(parts, near, far):
     vmem = pl.BlockSpec(memory_space=pltpu.VMEM)
     out = jax.ShapeDtypeStruct((HEAD_WIDTH, parts.shape[1]), BF16)
-    keys, values = pl.pallas_call(
+    keys, values, up = pl.pallas_call(
         sum_kernel,
-        out_shape=(out, out),
-        in_specs=[vmem],
-        out_specs=(vmem, vmem),
+        out_shape=(out, out, jax.ShapeDtypeStruct(near.shape, BF16)),
+        in_specs=[vmem] * 3,
+        out_specs=(vmem,) * 3,
+        compiler_params=pltpu.CompilerParams(vmem_limit_bytes=60 * 2**20),
         cost_estimate=LIGHT,
-        name="sum_parts",
-    )(parts)
-    return keys.T, values.T
+        name="final_sums",
+    )(parts, near, far)
+    return keys.T, values.T, up
 
 
 def mix_matrix(routes, gates, experts, capacity):
@@ -440,52 +441,56 @@
     shard_rows = weight.shape[0]
     half_rows = X_RING * shard_rows
 
-    steps = 1 - place[0] // experts
-    keys, pairs = experts * tokens, width // HEAD_WIDTH * tokens
+    always = place[0] < experts
 
     crossed = other_y(weight)
     near = lax.all_gather(weight, "dp", axis=0, tiled=True, axis_index_groups=X_GROUPS)
-
-    chips = experts // 2
-    (kv,) = as_one(
-        steps, lambda i: (over_chips(i, saved_key_rows, saved_value_rows),), (chips * tokens, PAIR)
-    )
-    crossed, kv, routes = lax.optimization_barrier((crossed, kv, routes))
-    kv = with_other_core(kv)
-    copies = repeated(crossed)
-    copies, slot_grads, inputs = lax.optimization_barrier((copies, hidden_grad[0, 0], expert_in[0, 0]))
-    far = over_x(copies)
-
-    def weight_term(half):
-        grads = lax.dynamic_slice_in_dim(slot_grads, half * half_rows, half_rows, 1)
-        return lax.dot_general(grads, inputs, TN, preferred_element_type=F32).astype(BF16)
+    slot_grads = hidden_grad[0, 0]
+
+    def first(keys, values, grads, inputs):
+        def weight_term(half):
+            part = lax.dynamic_slice_in_dim(grads, half * half_rows, half_rows, 1)
+            return lax.dot_general(part, inputs, TN, preferred_element_type=F32).astype(BF16)
+
+        return packed(keys, values), weight_term(1 - y), weight_term(y)
+
+    kv, term_far, term_near = as_one(
+        always, first, saved_key_rows, saved_value_rows, slot_grads, expert_in[0, 0]
+    )
+    kv = over_chips(kv)
+    crossed, routes, term_far, term_near = lax.optimization_barrier((crossed, routes, term_far, term_near))
+    far = x_pieces(crossed)
+
+    def second(kv, queries, norms):
+        kv = with_other_core(kv)
+        return kv, *attention_weights(place, queries, norms, kv)
+
+    kv, attend, low = as_one(always, second, kv, queries, log_sum_norm)
+    kv, attend, low, term_far, term_near, *far = lax.optimization_barrier(
+        (kv, attend, low, term_far, term_near, *far)
+    )
+    rows = over_ctx(back_product(line.astype(jnp.int32).reshape(1), slot_grads, near, far))
+    mix = mix_matrix(routes, gates, experts, capacity)
 
     def x_sum(term):
         return lax.psum_scatter(term, "dp", scatter_dimension=0, tiled=True, axis_index_groups=X_GROUPS)
 
-    attend, low = attention_weights(place, queries, log_sum_norm, kv)
-    far, attend, low, term_far, term_near = lax.optimization_barrier(
-        (far, attend, low, weight_term(1 - y), weight_term(y))
-    )
-    sum_far = x_sum(term_far)
+    sum_far = other_y(x_sum(term_far))
     sum_near = x_sum(term_near)
-    rows = over_ctx(back_product(line.astype(jnp.int32).reshape(1), slot_grads, near, far))
-    mix = mix_matrix(routes, gates, experts, capacity)
-
-    sum_far = other_y(sum_far)
-
-    def attention(i):
-        grad_hidden, total = key_value_grads(place + i, mix, rows, grad_out, attn_out, attend, low, kv)
+
+    def attention(mix, rows, grad_out, attn_out, attend, low, norms, kv):
+        grad_hidden, total = key_value_grads(place, mix, rows, grad_out, attn_out, attend, low, kv)
         parts = over_ctx(total)
-        query_gradient = query_grads(place + i, grad_hidden, attn_out, low, log_sum_norm, kv)
-        return grad_hidden, query_gradient, parts
+        return grad_hidden, query_grads(place, grad_hidden, attn_out, low, norms, kv), parts
 
     grad_hidden, query_gradient, parts = as_one(
-        steps, attention, (tokens, width), (tokens, width), (keys, PAIR)
-    )
-    key_gradient, value_gradient = sum_parts(parts.reshape(experts, tokens, PAIR))
-    grad_up = (sum_near.astype(F32) + sum_far.astype(F32)).astype(BF16).reshape(up_weight.shape)
-    return grad_hidden, query_gradient, key_gradient, value_gradient, grad_up
+        always, attention, mix, rows, grad_out, attn_out, attend, low, log_sum_norm, kv
+    )
+    parts, sum_far, sum_near = lax.optimization_barrier((parts, sum_far, sum_near))
+    key_gradient, value_gradient, grad_up = final_sums(
+        parts.reshape(experts, tokens, PAIR), sum_near, sum_far
+    )
+    return grad_hidden, query_gradient, key_gradient, value_gradient, grad_up.reshape(up_weight.shape)
 
 
 def solution(mesh):

time: 153 us -> 149 us (0.974)
  local copies, waits for them, and re-layouts: 9.4 us -> 2.76 us
  starting transfers between devices: 51 us -> 56.7 us
  other arithmetic: 3.37 us -> 0.63 us
  matrix products: 6.69 us -> 4.94 us
    ppermute x0 -> x3, waiting for transfers between devices: none -> 11 us  [along_x(): return lax.ppermute(shard, 'dp', order)]
    ppermute x0 -> x3, starting transfers between devices: none -> 10.5 us  [along_x(): return lax.ppermute(shard, 'dp', order)]
    all_to_all x1, waiting for transfers between devices: 10.1 us -> 0.01 us  [over_chips(): lax.all_to_all(copies, 'ctx', 0, 0, tiled=True, axis_index_groups=same_core)]
    all_to_all x1 -> x0, starting transfers between devices: 4.14 us -> none  [over_x(): lax.all_to_all(shard, 'dp', 0, 0, tiled=True, axis_index_groups=X_GROUPS)]
    unnamed x22 -> x20, local copies, waits for them, and re-layouts: 5.14 us -> 1.44 us
    pallas_call x1, Pallas kernels: 2.14 us -> 4.68 us  [back_product(): pl.pallas_call(back_kernel, out_shape=jax.ShapeDtypeStruct((grads.shape[0...]
    all_to_all x1 -> x0, waiting for transfers between devices: 2.13 us -> none  [over_x(): lax.all_to_all(shard, 'dp', 0, 0, tiled=True, axis_index_groups=X_GROUPS)]
    reshape x1 -> x0, other arithmetic: 2 us -> none  [body(): (sum_near.astype(F32) + sum_far.astype(F32)).astype(BF16)]
  transfers between devices with their start and end apart: 10 -> 12, of which waited for: 5 -> 6; matrix products, arithmetic and copies ran while one was open for 8% -> 5% of each run, Pallas kernels for 14% -> 14%
where the time goes in v2:
time: 149 us; the launch traced here: 148 us
  starting transfers between devices  56.7 us (38%)
  waiting for transfers between devices  46.5 us (31%)
  Pallas kernels  22.4 us (15%)
  between operations  14 us (9%)
  matrix products  4.94 us (3%)
  local copies, waits for them, and re-layouts  2.76 us (2%)
    all_to_all x2, waiting for transfers between devices, over_ctx(): return lax.all_to_all(shard, 'ctx', 0, 0, tiled=True)  18.1 us
    all_to_all x2, starting transfers between devices, over_ctx(): return lax.all_to_all(shard, 'ctx', 0, 0, tiled=True)  16.5 us
    ppermute x2, starting transfers between devices, other_y(): lax.ppermute(shard, 'dp', [(i, (i + X_RING) % (2 * X_RING)) for i in rang...  15.3 us
    reduce_scatter x2, waiting for transfers between devices, x_sum(): lax.psum_scatter(term, 'dp', scatter_dimension=0, tiled=True, axis_index_...  14.9 us
    pallas_call x3, Pallas kernels, call(): pl.pallas_call(kernel, out_shape=out_shape, grid_spec=pltpu.PrefetchScala...  13.9 us
    ppermute x3, waiting for transfers between devices, along_x(): return lax.ppermute(shard, 'dp', order)  11 us
    ppermute x3, starting transfers between devices, along_x(): return lax.ppermute(shard, 'dp', order)  10.5 us
    all_to_all x1, starting transfers between devices, over_chips(): lax.all_to_all(copies, 'ctx', 0, 0, tiled=True, axis_index_groups=same_core)  10.1 us
  transfers between devices with their start and end apart: 12, of which 6 were waited for; matrix products, arithmetic and copies ran while one was open for 5% of the time, Pallas kernels for 14%

profile of v2, /device:TPU:1, one launch (start us, length us, event | category | flops | bytes accessed | tf_op | source)
XLA Modules:
  0.0 148.0 jit_solution(1603159636461436894)
XLA Ops:
  7.2 0.0 all-gather.3.cloned.1.call-start
  7.2 0.7 all-gather.3.cloned.1.call-update
  7.9 8.3 %collective-permute-start.1 = (bf16[192,1024]{1,0:T(8,128)(2,1)}, bf16[192,1024]{1,0:T(8,128)(2,1)}, u32[]{:S(2)}, u32[]{:S(2)}) collective-permute-start(bf16[192,1024]{1,0:T(8,128)(2,1)} %bitcast.75), channel_id=1, source_target_pairs={{0,256},{64,320},{128,384},{192,448},{256,0},{320,64},{384,128},{4... | collective-permute-start | bytes 1179656 | tf_op jit(solution)/shard_map/ppermute | solution.py:27
  16.2 6.6 %conditional.3 = (bf16[1024,128]{1,0:T(8,128)(2,1)}, bf16[768,1024]{1,0:T(8,128)(2,1)S(1)}, bf16[768,1024]{1,0:T(8,128)(2,1)S(1)}) conditional(s32[]{:T(128)} %convert_element_type.36, () %tuple.37, (bf16[128,64]{0,1:T(8,128)(2,1)}, bf16[128,64]{0,1:T(8,128)(2,1)}, s32[]{:T(128)}, bf16[512,1536]{1,0:T(8,128)(2,1)}, ...), branch_computations={%region_0.1_spmd, %region_1.2_spmd.clone} | conditional | flops 1613234176 | bytes 6881491 | solution.py:342
  16.2 1.6 %pack.1 = bf16[1024,128]{1,0:T(8,128)(2,1)} custom-call(bf16[64,128]{1,0:T(8,128)(2,1)} %bitcast.77, bf16[64,128]{1,0:T(8,128)(2,1)} %bitcast.78), custom_call_target="tpu_custom_call" | custom-call | flops 1048576 | bytes 65536 | tf_op jit(solution)/shard_map/cond/branch_1_fun/pack/pallas_call | solution.py:356
  17.8 2.5 %convolution_convert_fusion.1 = bf16[768,1024]{1,0:T(8,128)(2,1)S(1)} fusion(bf16[1,1,512,1024]{3,2,1,0:T(8,128)(2,1)} %get-tuple-element.156, bf16[512,1536]{1,0:T(8,128)(2,1)} %get-tuple-element.150, s32[]{:T(128)S(6)} %select_n.64), kind=kOutput, calls=%fused_computation.4 | convolution fusion | flops 806092800 | bytes 3407876 | tf_op jit(solution)/shard_map/cond/branch_1_fun/dot_general | solution.py:453
  20.3 2.5 %convolution_convert_fusion = bf16[768,1024]{1,0:T(8,128)(2,1)S(1)} fusion(bf16[1,1,512,1024]{3,2,1,0:T(8,128)(2,1)} %get-tuple-element.156, bf16[512,1536]{1,0:T(8,128)(2,1)} %get-tuple-element.150, s32[]{:T(128)S(6)} %select_n.65), kind=kOutput, calls=%fused_computation.3 | convolution fusion | flops 806092800 | bytes 3407876 | tf_op jit(solution)/shard_map/cond/branch_1_fun/dot_general | solution.py:453
  22.8 10.1 %all-to-all-start.1 = ((bf16[8,128,128]{2,1,0:T(8,128)(2,1)}), bf16[8,128,128]{2,1,0:T(8,128)(2,1)S(1)}, u32[]{:S(2)}, u32[]{:S(2)}) async-start(bf16[8,128,128]{2,1,0:T(8,128)(2,1)} %bitcast.11), calls=%async_computation.1 | async-start | bytes 524288 | tf_op jit(solution)/shard_map/all_to_all | solution.py:369
  32.9 0.0 reduce-scatter.3.cloned.1.call-start
  32.9 3.1 %collective-permute-start.2 = (bf16[192,1024]{1,0:T(8,128)(2,1)}, bf16[192,1024]{1,0:T(8,128)(2,1)}, u32[]{:S(2)}, u32[]{:S(2)}) collective-permute-start(bf16[192,1024]{1,0:T(8,128)(2,1)} %collective-permute-done.1.rest_0_), channel_id=1, source_target_pairs={{0,64},{64,128},{128,192},{192,0},{256,320},{320,384},{384,448},{4... | collective-permute-start | bytes 1179656 | tf_op jit(solution)/shard_map/ppermute | solution.py:39
  36.0 4.4 %collective-permute-start.3 = (bf16[192,1024]{1,0:T(8,128)(2,1)}, bf16[192,1024]{1,0:T(8,128)(2,1)}, u32[]{:S(2)}, u32[]{:S(2)}) collective-permute-start(bf16[192,1024]{1,0:T(8,128)(2,1)} %collective-permute-done.1.rest_0_), channel_id=1, source_target_pairs={{0,128},{64,192},{128,0},{192,64},{256,384},{320,448},{384,256},{4... | collective-permute-start | bytes 1179656 | tf_op jit(solution)/shard_map/ppermute | solution.py:39
  40.4 3.1 %collective-permute-start.4 = (bf16[192,1024]{1,0:T(8,128)(2,1)}, bf16[192,1024]{1,0:T(8,128)(2,1)}, u32[]{:S(2)}, u32[]{:S(2)}) collective-permute-start(bf16[192,1024]{1,0:T(8,128)(2,1)} %collective-permute-done.1.rest_0_), channel_id=1, source_target_pairs={{0,192},{64,0},{128,64},{192,128},{256,448},{320,256},{384,320},{4... | collective-permute-start | bytes 1179656 | tf_op jit(solution)/shard_map/ppermute | solution.py:39
  43.5 9.6 %conditional.4 = (bf16[2048,128]{1,0:T(8,128)(2,1)}, bf16[2048,2048]{1,0:T(8,128)(2,1)}, bf16[2048,128]{1,0:T(8,128)(2,1)}) conditional(s32[]{:T(128)} %convert_element_type.36, () %tuple.36, (bf16[8,128,128]{2,1,0:T(8,128)(2,1)S(1)}, s32[1]{0:T(128)}, bf16[128,1024]{1,0:T(8,128)(2,1)}, f32[16,128]{1,0:T(8,128)S(1)}) %tuple.81), branch_computations={%region_3.4_spmd, %region_4.5_spmd} | conditional | flops 1572879 | bytes 9437214 | solution.py:342
  43.5 4.1 %collective-permute-start = (bf16[1024,128]{1,0:T(8,128)(2,1)S(1)}, bf16[1024,128]{1,0:T(8,128)(2,1)S(1)}, u32[]{:S(2)}, u32[]{:S(2)}) collective-permute-start(bf16[1024,128]{1,0:T(8,128)(2,1)S(1)} %bitcast.73), channel_id=1, source_target_pairs={{0,4},{4,0},{8,12},{12,8},{16,20},{20,16},{24,28},{28,24},{32,36},... | collective-permute-start | bytes 786440 | tf_op jit(solution)/shard_map/cond/branch_1_fun/ppermute | solution.py:374
  47.6 1.1 collective-permute-done
  48.8 0.1 pad_maximum_fusion
  48.9 0.9 copy.36
  49.7 3.4 %attend.1 = (bf16[2048,2048]{1,0:T(8,128)(2,1)}, bf16[2048,128]{1,0:T(8,128)(2,1)}) custom-call(s32[1]{0:T(128)} %get-tuple-element.44.place_ref, bf16[128,1024]{1,0:T(8,128)(2,1)S(1)} %copy-done.7, f32[16,128]{1,0:T(8,128)S(1)} %get-tuple-element.46.norm_ref, bf16[2048,128]{1,0:T(8,128)(2,1)} %bitcast.4.kv_ref), custom_call_target="tpu_custom_call" | custom-call | flops 1048576 | bytes 65536 | tf_op jit(solution)/shard_map/cond/branch_1_fun/attend/pallas_call | solution.py:242
  53.1 2.1 %collective-permute-done.2.rest_1_ = bf16[192,1024]{1,0:T(8,128)(2,1)} collective-permute-done((bf16[192,1024]{1,0:T(8,128)(2,1)}, bf16[192,1024]{1,0:T(8,128)(2,1)}, u32[]{:S(2)}, u32[]{:S(2)}) %collective-permute-start.2) | collective-permute-done | bytes 393248 | tf_op jit(solution)/shard_map/ppermute | solution.py:39
  55.2 8.8 %collective-permute-done.3.rest_2_ = bf16[192,1024]{1,0:T(8,128)(2,1)} collective-permute-done((bf16[192,1024]{1,0:T(8,128)(2,1)}, bf16[192,1024]{1,0:T(8,128)(2,1)}, u32[]{:S(2)}, u32[]{:S(2)}) %collective-permute-start.3) | collective-permute-done | bytes 393248 | tf_op jit(solution)/shard_map/ppermute | solution.py:39
  64.0 0.0 reduce-scatter.3.cloned.1.call-update
  64.1 0.0 reduce-scatter.5.cloned.1.call-start
  64.1 0.7 reduce-scatter.5.cloned.1.call-update
  64.8 0.0 all-gather.3.cloned.1.call-done
  64.8 0.6 copy-done.2
  65.5 4.7 %back_rows.1 = bf16[512,1024]{1,0:T(8,128)(2,1)} custom-call(s32[1]{0:T(128)} %bitcast.8.line_ref, bf16[512,1536]{1,0:T(8,128)(2,1)S(1)} %bitcast.71, bf16[768,1024]{1,0:T(8,128)(2,1)} %bitcast.72, bf16[192,1024]{1,0:T(8,128)(2,1)} %collective-permute-done.1.rest_0_, bf16[192,1024]{1,0:T(8,128)(2,1)} %collective-permute-done.2.rest_1_, ...), custom_call_target="tpu_custom_call" | custom-call | flops 1048576 | bytes 65536 | tf_op jit(solution)/shard_map/back_rows/pallas_call | solution.py:72
  70.1 0.0 copy-start.10
  70.1 0.0 copy-start.9
  70.2 0.0 copy-start.3
  70.2 0.0 copy-start.5
  70.2 8.5 %all-to-all-start.2 = ((bf16[16,32,1024]{2,1,0:T(8,128)(2,1)}), bf16[16,32,1024]{2,1,0:T(8,128)(2,1)S(1)}, u32[]{:S(2)}, u32[]{:S(2)}) async-start(bf16[16,32,1024]{2,1,0:T(8,128)(2,1)} %bitcast.69), calls=%async_computation.2 | async-start | bytes 2097152 | tf_op jit(solution)/shard_map/all_to_all | solution.py:90
  78.7 0.1 copy.37
  78.9 0.1 eq.33
  79.0 0.2 convert_reduce_fusion
  79.2 0.1 reduce_sum.12
  79.3 0.1 copy.38
  79.4 14.9 %reduce-scatter.3.cloned.1.call-done = bf16[192,1024]{1,0:T(8,128)(2,1)} async-done(((bf16[768,1024]{1,0:T(8,128)(2,1)}), bf16[192,1024]{1,0:T(8,128)(2,1)}) %reduce-scatter.3.cloned.1.call-update) | async-done | bytes 393232 | tf_op jit(solution)/shard_map/reduce_scatter | solution.py:476
  94.2 7.0 %collective-permute-start.5 = (bf16[192,1024]{1,0:T(8,128)(2,1)}, bf16[192,1024]{1,0:T(8,128)(2,1)S(1)}, u32[]{:S(2)}, u32[]{:S(2)}) collective-permute-start(bf16[192,1024]{1,0:T(8,128)(2,1)} %reduce-scatter.3.cloned.1.call-done), channel_id=1, source_target_pairs={{0,256},{64,320},{128,384},{192,448},{256,0},{320,64},{384,128},{4... | collective-permute-start | bytes 1179656 | tf_op jit(solution)/shard_map/ppermute | solution.py:27
  101.3 0.1 iota_compare_fusion
  101.4 0.2 fusion.13
  101.7 5.2 %all-to-all-done.2 = bf16[16,32,1024]{2,1,0:T(8,128)(2,1)S(1)} async-done(((bf16[16,32,1024]{2,1,0:T(8,128)(2,1)}), bf16[16,32,1024]{2,1,0:T(8,128)(2,1)S(1)}, u32[]{:S(2)}, u32[]{:S(2)}) %all-to-all-start.2) | async-done | bytes 1048608 | tf_op jit(solution)/shard_map/all_to_all | solution.py:90
  106.9 31.5 %conditional.5 = (bf16[128,1024]{1,0:T(8,128)(2,1)}, bf16[128,1024]{1,0:T(8,128)(2,1)S(1)}, bf16[2048,128]{1,0:T(8,128)(2,1)}) conditional(s32[]{:T(128)} %convert_element_type.36, () %tuple.35, (bf16[16,32,1024]{2,1,0:T(8,128)(2,1)S(1)}, s32[1]{0:T(128)}, bf16[384,512]{1,0:T(8,128)(2,1)S(1)}, bf16[128,1024]{1,0:T(8,128)(2,1)S(1)}, ...), branch_computations={%region_5.6_spmd, %region_6.7_spmd} | conditional | flops 2097152 | bytes 1703992 | solution.py:342
  106.9 6.0 %key_value_grads.1 = (bf16[128,1024]{1,0:T(8,128)(2,1)}, bf16[2048,128]{1,0:T(8,128)(2,1)}) custom-call(s32[1]{0:T(128)} %get-tuple-element.49.place_ref, bf16[384,512]{1,0:T(8,128)(2,1)S(1)} %get-tuple-element.50.mix_ref, bf16[512,1024]{1,0:T(8,128)(2,1)S(1)} %bitcast.68, bf16[128,1024]{1,0:T(8,128)(2,1)S(1)} %get-tuple-element.148.grad_out_ref, ...), custom_call_target="tpu_custom_call" | custom-call | flops 1048576 | bytes 65536 | tf_op jit(solution)/shard_map/cond/branch_1_fun/key_value_grads/pallas_call | solution.py:242
  112.9 8.0 %all-to-all-start = ((bf16[16,128,128]{2,1,0:T(8,128)(2,1)}), bf16[16,128,128]{2,1,0:T(8,128)(2,1)}, u32[]{:S(2)}, u32[]{:S(2)}) async-start(bf16[16,128,128]{2,1,0:T(8,128)(2,1)} %bitcast.74), calls=%async_computation | async-start | bytes 1048576 | tf_op jit(solution)/shard_map/cond/branch_1_fun/all_to_all | solution.py:90
  120.9 4.5 %query_grads.1 = bf16[128,1024]{1,0:T(8,128)(2,1)S(1)} custom-call(s32[1]{0:T(128)} %get-tuple-element.49.place_ref, bf16[128,1024]{1,0:T(8,128)(2,1)} %get-tuple-element.203.hidden_ref, bf16[128,1024]{1,0:T(8,128)(2,1)S(1)} %get-tuple-element.149.out_ref, bf16[2048,128]{1,0:T(8,128)(2,1)} %get-tuple-element.55.low_ref, ...), custom_call_target="tpu_custom_call" | custom-call | flops 1048576 | bytes 65536 | tf_op jit(solution)/shard_map/cond/branch_1_fun/query_grads/pallas_call | solution.py:242
  125.5 12.9 %all-to-all-done = bf16[16,128,128]{2,1,0:T(8,128)(2,1)} async-done(((bf16[16,128,128]{2,1,0:T(8,128)(2,1)}), bf16[16,128,128]{2,1,0:T(8,128)(2,1)}, u32[]{:S(2)}, u32[]{:S(2)}) %all-to-all-start) | async-done | bytes 524320 | tf_op jit(solution)/shard_map/cond/branch_1_fun/all_to_all | solution.py:90
  138.4 0.8 copy-done.4
  139.2 2.3 %final_sums.1 = (bf16[64,128]{1,0:T(8,128)(2,1)}, bf16[64,128]{1,0:T(8,128)(2,1)}, bf16[192,1024]{1,0:T(8,128)(2,1)}) custom-call(bf16[16,128,128]{2,1,0:T(8,128)(2,1)} %bitcast.23.parts_ref, bf16[192,1024]{1,0:T(8,128)(2,1)} %reduce-scatter.5.cloned.1.call-done.near_ref, bf16[192,1024]{1,0:T(8,128)(2,1)} %copy-done.4), custom_call_target="tpu_custom_call" | custom-call | flops 1048576 | bytes 65536 | tf_op jit(solution)/shard_map/final_sums/pallas_call | solution.py:391
  (27 shorter events, 0.1 us)
Async XLA Ops:
  7.2 57.7 %all-gather.3.cloned.1.call-start = ((), (), s32[]{:S(2)}) async-start(), calls=%async_computation.7 | async-start | bytes 1966080 | tf_op jit(solution)/shard_map/all_gather | solution.py:447
  7.9 25.0 %collective-permute-start.1 = (bf16[192,1024]{1,0:T(8,128)(2,1)}, bf16[192,1024]{1,0:T(8,128)(2,1)}, u32[]{:S(2)}, u32[]{:S(2)}) collective-permute-start(bf16[192,1024]{1,0:T(8,128)(2,1)} %bitcast.75), channel_id=1, source_target_pairs={{0,256},{64,320},{128,384},{192,448},{256,0},{320,64},{384,128},{4... | collective-permute-start | bytes 1179656 | tf_op jit(solution)/shard_map/ppermute | solution.py:27
  16.2 27.3 %copy-start.8 = (f32[16,128]{1,0:T(8,128)S(1)}, f32[16,128]{1,0:T(8,128)}, u32[]{:S(2)}) copy-start(f32[16,128]{1,0:T(8,128)} %param.21) | copy-start | bytes 24580
  22.8 20.7 %copy-start = (bf16[768,1024]{1,0:T(8,128)(2,1)}, bf16[768,1024]{1,0:T(8,128)(2,1)S(1)}, u32[]{:S(2)}) copy-start(bf16[768,1024]{1,0:T(8,128)(2,1)S(1)} %get-tuple-element.113) | copy-start | bytes 4718596
  22.8 20.7 %copy-start.1 = (bf16[768,1024]{1,0:T(8,128)(2,1)}, bf16[768,1024]{1,0:T(8,128)(2,1)S(1)}, u32[]{:S(2)}) copy-start(bf16[768,1024]{1,0:T(8,128)(2,1)S(1)} %get-tuple-element.114) | copy-start | bytes 4718596
  22.8 20.7 %all-to-all-start.1 = ((bf16[8,128,128]{2,1,0:T(8,128)(2,1)}), bf16[8,128,128]{2,1,0:T(8,128)(2,1)S(1)}, u32[]{:S(2)}, u32[]{:S(2)}) async-start(bf16[8,128,128]{2,1,0:T(8,128)(2,1)} %bitcast.11), calls=%async_computation.1 | async-start | bytes 524288 | tf_op jit(solution)/shard_map/all_to_all | solution.py:369
  32.9 61.4 %reduce-scatter.3.cloned.1.call-start = ((), (), s32[]{:S(2)}) async-start(), calls=%async_computation.5 | async-start | bytes 1966080 | tf_op jit(solution)/shard_map/reduce_scatter | solution.py:476
  32.9 22.3 %collective-permute-start.2 = (bf16[192,1024]{1,0:T(8,128)(2,1)}, bf16[192,1024]{1,0:T(8,128)(2,1)}, u32[]{:S(2)}, u32[]{:S(2)}) collective-permute-start(bf16[192,1024]{1,0:T(8,128)(2,1)} %collective-permute-done.1.rest_0_), channel_id=1, source_target_pairs={{0,64},{64,128},{128,192},{192,0},{256,320},{320,384},{384,448},{4... | collective-permute-start | bytes 1179656 | tf_op jit(solution)/shard_map/ppermute | solution.py:39
  36.0 28.0 %collective-permute-start.3 = (bf16[192,1024]{1,0:T(8,128)(2,1)}, bf16[192,1024]{1,0:T(8,128)(2,1)}, u32[]{:S(2)}, u32[]{:S(2)}) collective-permute-start(bf16[192,1024]{1,0:T(8,128)(2,1)} %collective-permute-done.1.rest_0_), channel_id=1, source_target_pairs={{0,128},{64,192},{128,0},{192,64},{256,384},{320,448},{384,256},{4... | collective-permute-start | bytes 1179656 | tf_op jit(solution)/shard_map/ppermute | solution.py:39
  40.4 23.6 %collective-permute-start.4 = (bf16[192,1024]{1,0:T(8,128)(2,1)}, bf16[192,1024]{1,0:T(8,128)(2,1)}, u32[]{:S(2)}, u32[]{:S(2)}) collective-permute-start(bf16[192,1024]{1,0:T(8,128)(2,1)} %collective-permute-done.1.rest_0_), channel_id=1, source_target_pairs={{0,192},{64,0},{128,64},{192,128},{256,448},{320,256},{384,320},{4... | collective-permute-start | bytes 1179656 | tf_op jit(solution)/shard_map/ppermute | solution.py:39
  43.5 5.2 %collective-permute-start = (bf16[1024,128]{1,0:T(8,128)(2,1)S(1)}, bf16[1024,128]{1,0:T(8,128)(2,1)S(1)}, u32[]{:S(2)}, u32[]{:S(2)}) collective-permute-start(bf16[1024,128]{1,0:T(8,128)(2,1)S(1)} %bitcast.73), channel_id=1, source_target_pairs={{0,4},{4,0},{8,12},{12,8},{16,20},{20,16},{24,28},{28,24},{32,36},... | collective-permute-start | bytes 786440 | tf_op jit(solution)/shard_map/cond/branch_1_fun/ppermute | solution.py:374
  48.8 1.0 copy-start.7
  64.0 1.4 copy-start.2
  64.1 74.3 %reduce-scatter.5.cloned.1.call-start = ((), (), s32[]{:S(2)}) async-start(), calls=%async_computation.6 | async-start | bytes 1966080 | tf_op jit(solution)/shard_map/reduce_scatter | solution.py:476
  70.1 8.5 %copy-start.10 = (f32[128,2]{0,1:T(2,128)S(1)}, f32[128,2]{0,1:T(2,128)}, u32[]{:S(2)}) copy-start(f32[128,2]{0,1:T(2,128)} %param.24) | copy-start | bytes 3076
  70.1 8.6 %copy-start.9 = (s32[128,2]{0,1:T(2,128)S(1)}, s32[128,2]{0,1:T(2,128)}, u32[]{:S(2)}) copy-start(s32[128,2]{0,1:T(2,128)} %param.23) | copy-start | bytes 3076
  70.2 36.7 %copy-start.3 = (bf16[128,1024]{1,0:T(8,128)(2,1)S(1)}, bf16[128,1024]{1,0:T(8,128)(2,1)}, u32[]{:S(2)}) copy-start(bf16[128,1024]{1,0:T(8,128)(2,1)} %param.20) | copy-start | bytes 786436
  70.2 36.7 %copy-start.5 = (bf16[128,1024]{1,0:T(8,128)(2,1)S(1)}, bf16[128,1024]{1,0:T(8,128)(2,1)}, u32[]{:S(2)}) copy-start(bf16[128,1024]{1,0:T(8,128)(2,1)} %param.22) | copy-start | bytes 786436
  70.2 36.7 %all-to-all-start.2 = ((bf16[16,32,1024]{2,1,0:T(8,128)(2,1)}), bf16[16,32,1024]{2,1,0:T(8,128)(2,1)S(1)}, u32[]{:S(2)}, u32[]{:S(2)}) async-start(bf16[16,32,1024]{2,1,0:T(8,128)(2,1)} %bitcast.69), calls=%async_computation.2 | async-start | bytes 2097152 | tf_op jit(solution)/shard_map/all_to_all | solution.py:90
  94.2 44.1 %collective-permute-start.5 = (bf16[192,1024]{1,0:T(8,128)(2,1)}, bf16[192,1024]{1,0:T(8,128)(2,1)S(1)}, u32[]{:S(2)}, u32[]{:S(2)}) collective-permute-start(bf16[192,1024]{1,0:T(8,128)(2,1)} %reduce-scatter.3.cloned.1.call-done), channel_id=1, source_target_pairs={{0,256},{64,320},{128,384},{192,448},{256,0},{320,64},{384,128},{4... | collective-permute-start | bytes 1179656 | tf_op jit(solution)/shard_map/ppermute | solution.py:27
  112.9 25.5 %all-to-all-start = ((bf16[16,128,128]{2,1,0:T(8,128)(2,1)}), bf16[16,128,128]{2,1,0:T(8,128)(2,1)}, u32[]{:S(2)}, u32[]{:S(2)}) async-start(bf16[16,128,128]{2,1,0:T(8,128)(2,1)} %bitcast.74), calls=%async_computation | async-start | bytes 1048576 | tf_op jit(solution)/shard_map/cond/branch_1_fun/all_to_all | solution.py:90
  138.4 3.1 %copy-start.6 = (bf16[128,1024]{1,0:T(8,128)(2,1)}, bf16[128,1024]{1,0:T(8,128)(2,1)S(1)}, u32[]{:S(2)}) copy-start(bf16[128,1024]{1,0:T(8,128)(2,1)S(1)} %get-tuple-element.89) | copy-start | bytes 786436
  138.4 0.8 copy-start.4
Sparse Core Ops, SparseCore 0:
  10.1 45.0 all-gather.2
  64.2 30.0 reduce-scatter.2
  97.1 30.7 reduce-scatter.4

commit v3 on v2

--- a/solution.py
+++ b/solution.py
@@ -9,9 +9,8 @@
 
 HEAD_WIDTH = 64
 PAIR = 2 * HEAD_WIDTH
-KEY_TILE = 256
+KEY_TILE = 512
 ROW_TILE = 1024
-QUERY_KEY_TILE = 512
 QUERY_ROW_TILE = 512
 X_RING = 4
 F32 = jnp.float32
@@ -47,22 +46,28 @@
     far, (out_ref, grads, weight, back, sems) = rest[:X_RING], rest[X_RING:]
     x, y = line_ref[0] % X_RING, line_ref[0] // X_RING
     half, rows = near_ref.shape[0], far[0].shape[0]
-    near_rows = pl.ds(pl.multiple_of(y * half, half), half)
-    pairs = [(grads_ref, grads), (near_ref, weight.at[near_rows])]
+    pieces = [(near_ref, y * half, half)]
     for by, ref in enumerate(far):
-        start = (1 - y) * half + (x + X_RING - by) % X_RING * rows
-        pairs.append((ref, weight.at[pl.ds(pl.multiple_of(start, rows), rows)]))
-    for copy in run_copies(pairs, sems):
-        copy.wait()
-    parts = sems.shape[0] - len(pairs)
-    width = out_ref.shape[1] // parts
-    copies = []
-    for i in range(parts):
-        at = slice(i * width, (i + 1) * width)
+        pieces.append((ref, (1 - y) * half + (x + X_RING - by) % X_RING * rows, rows))
+    width = out_ref.shape[1] // 2
+    sides = [slice(i * width, (i + 1) * width) for i in range(2)]
+    arriving, used = [], 1
+    copies = run_copies([(grads_ref, grads)], sems)
+    for at in sides:
+        pairs = [
+            (ref.at[:, at], weight.at[pl.ds(pl.multiple_of(start, rows), size), at])
+            for ref, start, size in pieces
+        ]
+        arriving.append(run_copies(pairs, sems.at[pl.ds(used, len(pairs))]))
+        used += len(pairs)
+    copies[0].wait()
+    leaving = []
+    for i, at in enumerate(sides):
+        for copy in arriving[i]:
+            copy.wait()
         back[:, at] = jnp.dot(grads[...], weight[:, at], preferred_element_type=F32).astype(BF16)
-        copies.append(pltpu.make_async_copy(back.at[:, at], out_ref.at[:, at], sems.at[len(pairs) + i]))
-        copies[-1].start()
-    for copy in copies:
+        leaving += run_copies([(back.at[:, at], out_ref.at[:, at])], sems.at[pl.ds(used + i, 1)])
+    for copy in leaving:
         copy.wait()
 
 
@@ -78,7 +83,7 @@
             pltpu.VMEM(grads.shape, BF16),
             pltpu.VMEM((depth, width), BF16),
             pltpu.VMEM((grads.shape[0], width), BF16),
-            pltpu.SemaphoreType.DMA((2 + X_RING + 4,)),
+            pltpu.SemaphoreType.DMA((1 + 2 * (1 + X_RING) + 2,)),
         ],
         compiler_params=pltpu.CompilerParams(vmem_limit_bytes=60 * 2**20),
         cost_estimate=LIGHT,
@@ -143,14 +148,19 @@
 
 def key_value_kernel(
     place_ref, mix_ref, rows_ref, grad_out_ref, out_ref, attend_ref, low_ref, kv_ref,
-    hidden_ref, sum_ref, high, delta,
+    hidden_ref, sum_ref, high, delta, held, sems,
 ):
     tokens, width = grad_out_ref.shape
-    j, place = pl.program_id(0), place_ref[0]
-    last = last_tile(place, KEY_TILE, tokens)
-
-    @pl.when(j == 0)
-    def _():
+    last = last_tile(place_ref[0], KEY_TILE, tokens)
+
+    def fetch(j):
+        return pltpu.make_async_copy(attend_ref.at[tile_rows(j, KEY_TILE)], held.at[j], sems.at[j])
+
+    def ahead(j, carry):
+        fetch(j).start()
+        return carry
+
+    def prepare():
         first = lax.broadcasted_iota(jnp.int32, (tokens, PAIR), 1) < HEAD_WIDTH
         mixed = jnp.dot(mix_ref[...], rows_ref[...], preferred_element_type=F32)
         hidden = (
@@ -167,23 +177,30 @@
             delta[:, even] = jnp.sum(prod[:HEAD_WIDTH], axis=0, keepdims=True)
             delta[:, odd] = jnp.sum(prod[HEAD_WIDTH:], axis=0, keepdims=True)
 
-    @pl.when(j <= last)
-    def _():
+    lax.fori_loop(0, last + 1, ahead, 0)
+    prepare()
+
+    def tile(j, carry):
+        fetch(j).wait()
         kv = kv_ref[tile_rows(j, KEY_TILE), :]
         total = jnp.zeros((KEY_TILE, PAIR), F32)
         for r in range(high.shape[0] // ROW_TILE):
             at = slice(r * ROW_TILE, (r + 1) * ROW_TILE)
             g = high[at, :]
-            attend = attend_ref[:, at]
+            attend = held[j, :, at]
             prob = lax.dot_general(kv, g, NT, preferred_element_type=F32)
             score_grad = (attend.astype(F32) * (prob - delta[:, at])).astype(BF16)
             total = total + jnp.dot(score_grad, low_ref[at, :], preferred_element_type=F32)
             total = total + jnp.dot(attend, g, preferred_element_type=F32)
-        sum_ref[...] = total.astype(BF16)
-
-    @pl.when(j > last)
-    def _():
-        sum_ref[...] = jnp.zeros_like(sum_ref)
+        sum_ref[tile_rows(j, KEY_TILE), :] = total.astype(BF16)
+        return carry
+
+    def empty(j, carry):
+        sum_ref[tile_rows(j, KEY_TILE), :] = jnp.zeros((KEY_TILE, PAIR), BF16)
+        return carry
+
+    lax.fori_loop(0, last + 1, tile, 0)
+    lax.fori_loop(last + 1, kv_ref.shape[0] // KEY_TILE, empty, 0)
 
 
 def query_kernel(
@@ -191,7 +208,7 @@
 ):
     tokens, width = hidden_ref.shape
     j, place = pl.program_id(0), place_ref[0]
-    last = last_tile(place, QUERY_KEY_TILE, tokens)
+    last = last_tile(place, KEY_TILE, tokens)
     first = lax.broadcasted_iota(jnp.int32, (tokens, PAIR), 1) < HEAD_WIDTH
 
     @pl.when(j == 0)
@@ -210,13 +227,13 @@
         total[...] = jnp.zeros_like(total)
 
     def tile(masked):
-        kv = kv_ref[tile_rows(j, QUERY_KEY_TILE), :]
+        kv = kv_ref[tile_rows(j, KEY_TILE), :]
         for r in range(high.shape[0] // QUERY_ROW_TILE):
             at = slice(r * QUERY_ROW_TILE, (r + 1) * QUERY_ROW_TILE)
             scores = lax.dot_general(low_ref[at, :], kv, NT, preferred_element_type=F32)
             attend = jnp.exp(scores - norm[at, :])
             if masked:
-                key_pos = j * QUERY_KEY_TILE + lax.broadcasted_iota(jnp.int32, attend.shape, 1)
+                key_pos = j * KEY_TILE + lax.broadcasted_iota(jnp.int32, attend.shape, 1)
                 token = lax.broadcasted_iota(jnp.int32, attend.shape, 0) % tokens
                 attend = jnp.where(key_pos <= place * tokens + token, attend, 0.0)
             prob = lax.dot_general(high[at, :], kv, NT, preferred_element_type=F32)
@@ -287,12 +304,17 @@
     return call(
         key_value_kernel,
         "key_value_grads",
-        keys // KEY_TILE,
+        1,
         [whole(mix), whole(rows), whole(grad_out), whole(attn_out)]
-        + [pl.BlockSpec((KEY_TILE, lines), attend_block(tokens)), whole(low), whole(kv)],
-        (whole(out[0]), pl.BlockSpec((KEY_TILE, PAIR), lambda j, place: (j, 0))),
+        + [pl.BlockSpec(memory_space=pl.ANY), whole(low), whole(kv)],
+        (whole(out[0]), whole(out[1])),
         out,
-        [pltpu.VMEM((lines, PAIR), BF16), pltpu.VMEM((1, lines), F32)],
+        [
+            pltpu.VMEM((lines, PAIR), BF16),
+            pltpu.VMEM((1, lines), F32),
+            pltpu.VMEM((keys // KEY_TILE, KEY_TILE, lines), BF16),
+            pltpu.SemaphoreType.DMA((keys // KEY_TILE,)),
+        ],
         3,
         keys * lines,
         place,
@@ -312,7 +334,7 @@
     return call(
         query_kernel,
         "query_grads",
-        keys // QUERY_KEY_TILE,
+        keys // KEY_TILE,
         [whole(x) for x in (hidden, attn_out, low, norms, kv)],
         whole(out),
         out,

time: 149 us -> 151 us (1.013)
  starting transfers between devices: 56.7 us -> 59.1 us
    all_to_all x2, starting transfers between devices: 16.5 us -> 18.9 us  [over_ctx(): return lax.all_to_all(shard, 'ctx', 0, 0, tiled=True)]
where the time goes in v3:
time: 151 us; the launch traced here: 150 us
  starting transfers between devices  59.1 us (39%)
  waiting for transfers between devices  46 us (30%)
  Pallas kernels  22.8 us (15%)
  between operations  14 us (9%)
  matrix products  4.94 us (3%)
  local copies, waits for them, and re-layouts  2.76 us (2%)
    all_to_all x2, starting transfers between devices, over_ctx(): return lax.all_to_all(shard, 'ctx', 0, 0, tiled=True)  18.9 us
    all_to_all x2, waiting for transfers between devices, over_ctx(): return lax.all_to_all(shard, 'ctx', 0, 0, tiled=True)  17.8 us
    ppermute x2, starting transfers between devices, other_y(): lax.ppermute(shard, 'dp', [(i, (i + X_RING) % (2 * X_RING)) for i in rang...  15.3 us
    reduce_scatter x2, waiting for transfers between devices, x_sum(): lax.psum_scatter(term, 'dp', scatter_dimension=0, tiled=True, axis_index_...  15.2 us
    pallas_call x3, Pallas kernels, call(): pl.pallas_call(kernel, out_shape=out_shape, grid_spec=pltpu.PrefetchScala...  14.6 us
    ppermute x3, starting transfers between devices, along_x(): return lax.ppermute(shard, 'dp', order)  10.5 us
    ppermute x3, waiting for transfers between devices, along_x(): return lax.ppermute(shard, 'dp', order)  10.4 us
    all_to_all x1, starting transfers between devices, over_chips(): lax.all_to_all(copies, 'ctx', 0, 0, tiled=True, axis_index_groups=same_core)  10.1 us
  transfers between devices with their start and end apart: 12, of which 6 were waited for; matrix products, arithmetic and copies ran while one was open for 5% of the time, Pallas kernels for 14%

profile of v3, /device:TPU:1, one launch (start us, length us, event | category | flops | bytes accessed | tf_op | source)
XLA Modules:
  0.0 150.3 jit_solution(7083033405080590127)
XLA Ops:
  7.2 0.0 all-gather.3.cloned.1.call-start
  7.2 0.7 all-gather.3.cloned.1.call-update
  7.9 8.3 %collective-permute-start.1 = (bf16[192,1024]{1,0:T(8,128)(2,1)}, bf16[192,1024]{1,0:T(8,128)(2,1)}, u32[]{:S(2)}, u32[]{:S(2)}) collective-permute-start(bf16[192,1024]{1,0:T(8,128)(2,1)} %bitcast.75), channel_id=1, source_target_pairs={{0,256},{64,320},{128,384},{192,448},{256,0},{320,64},{384,128},{4... | collective-permute-start | bytes 1179656 | tf_op jit(solution)/shard_map/ppermute | solution.py:26
  16.2 6.6 %conditional.3 = (bf16[1024,128]{1,0:T(8,128)(2,1)}, bf16[768,1024]{1,0:T(8,128)(2,1)S(1)}, bf16[768,1024]{1,0:T(8,128)(2,1)S(1)}) conditional(s32[]{:T(128)} %convert_element_type.36, () %tuple.37, (bf16[128,64]{0,1:T(8,128)(2,1)}, bf16[128,64]{0,1:T(8,128)(2,1)}, s32[]{:T(128)}, bf16[512,1536]{1,0:T(8,128)(2,1)}, ...), branch_computations={%region_0.1_spmd, %region_1.2_spmd.clone} | conditional | flops 1613234176 | bytes 6881491 | solution.py:364
  16.2 1.6 %pack.1 = bf16[1024,128]{1,0:T(8,128)(2,1)} custom-call(bf16[64,128]{1,0:T(8,128)(2,1)} %bitcast.77, bf16[64,128]{1,0:T(8,128)(2,1)} %bitcast.78), custom_call_target="tpu_custom_call" | custom-call | flops 1048576 | bytes 65536 | tf_op jit(solution)/shard_map/cond/branch_1_fun/pack/pallas_call | solution.py:378
  17.8 2.5 %convolution_convert_fusion.1 = bf16[768,1024]{1,0:T(8,128)(2,1)S(1)} fusion(bf16[1,1,512,1024]{3,2,1,0:T(8,128)(2,1)} %get-tuple-element.156, bf16[512,1536]{1,0:T(8,128)(2,1)} %get-tuple-element.150, s32[]{:T(128)S(6)} %select_n.64), kind=kOutput, calls=%fused_computation.4 | convolution fusion | flops 806092800 | bytes 3407876 | tf_op jit(solution)/shard_map/cond/branch_1_fun/dot_general | solution.py:475
  20.3 2.5 %convolution_convert_fusion = bf16[768,1024]{1,0:T(8,128)(2,1)S(1)} fusion(bf16[1,1,512,1024]{3,2,1,0:T(8,128)(2,1)} %get-tuple-element.156, bf16[512,1536]{1,0:T(8,128)(2,1)} %get-tuple-element.150, s32[]{:T(128)S(6)} %select_n.65), kind=kOutput, calls=%fused_computation.3 | convolution fusion | flops 806092800 | bytes 3407876 | tf_op jit(solution)/shard_map/cond/branch_1_fun/dot_general | solution.py:475
  22.8 10.1 %all-to-all-start.1 = ((bf16[8,128,128]{2,1,0:T(8,128)(2,1)}), bf16[8,128,128]{2,1,0:T(8,128)(2,1)S(1)}, u32[]{:S(2)}, u32[]{:S(2)}) async-start(bf16[8,128,128]{2,1,0:T(8,128)(2,1)} %bitcast.11), calls=%async_computation.1 | async-start | bytes 524288 | tf_op jit(solution)/shard_map/all_to_all | solution.py:391
  32.9 0.0 reduce-scatter.3.cloned.1.call-start
  32.9 3.1 %collective-permute-start.2 = (bf16[192,1024]{1,0:T(8,128)(2,1)}, bf16[192,1024]{1,0:T(8,128)(2,1)}, u32[]{:S(2)}, u32[]{:S(2)}) collective-permute-start(bf16[192,1024]{1,0:T(8,128)(2,1)} %collective-permute-done.1.rest_0_), channel_id=1, source_target_pairs={{0,64},{64,128},{128,192},{192,0},{256,320},{320,384},{384,448},{4... | collective-permute-start | bytes 1179656 | tf_op jit(solution)/shard_map/ppermute | solution.py:38
  36.0 4.4 %collective-permute-start.3 = (bf16[192,1024]{1,0:T(8,128)(2,1)}, bf16[192,1024]{1,0:T(8,128)(2,1)}, u32[]{:S(2)}, u32[]{:S(2)}) collective-permute-start(bf16[192,1024]{1,0:T(8,128)(2,1)} %collective-permute-done.1.rest_0_), channel_id=1, source_target_pairs={{0,128},{64,192},{128,0},{192,64},{256,384},{320,448},{384,256},{4... | collective-permute-start | bytes 1179656 | tf_op jit(solution)/shard_map/ppermute | solution.py:38
  40.4 3.1 %collective-permute-start.4 = (bf16[192,1024]{1,0:T(8,128)(2,1)}, bf16[192,1024]{1,0:T(8,128)(2,1)}, u32[]{:S(2)}, u32[]{:S(2)}) collective-permute-start(bf16[192,1024]{1,0:T(8,128)(2,1)} %collective-permute-done.1.rest_0_), channel_id=1, source_target_pairs={{0,192},{64,0},{128,64},{192,128},{256,448},{320,256},{384,320},{4... | collective-permute-start | bytes 1179656 | tf_op jit(solution)/shard_map/ppermute | solution.py:38
  43.5 10.1 %conditional.4 = (bf16[2048,128]{1,0:T(8,128)(2,1)}, bf16[2048,2048]{1,0:T(8,128)(2,1)}, bf16[2048,128]{1,0:T(8,128)(2,1)}) conditional(s32[]{:T(128)} %convert_element_type.36, () %tuple.36, (bf16[8,128,128]{2,1,0:T(8,128)(2,1)S(1)}, s32[1]{0:T(128)}, bf16[128,1024]{1,0:T(8,128)(2,1)}, f32[16,128]{1,0:T(8,128)S(1)}) %tuple.81), branch_computations={%region_3.4_spmd, %region_4.5_spmd} | conditional | flops 1572879 | bytes 9437214 | solution.py:364
  43.5 4.1 %collective-permute-start = (bf16[1024,128]{1,0:T(8,128)(2,1)S(1)}, bf16[1024,128]{1,0:T(8,128)(2,1)S(1)}, u32[]{:S(2)}, u32[]{:S(2)}) collective-permute-start(bf16[1024,128]{1,0:T(8,128)(2,1)S(1)} %bitcast.73), channel_id=1, source_target_pairs={{0,4},{4,0},{8,12},{12,8},{16,20},{20,16},{24,28},{28,24},{32,36},... | collective-permute-start | bytes 786440 | tf_op jit(solution)/shard_map/cond/branch_1_fun/ppermute | solution.py:396
  47.6 1.1 collective-permute-done
  48.8 0.1 pad_maximum_fusion
  48.9 0.9 copy.36
  49.7 3.9 %attend.1 = (bf16[2048,2048]{1,0:T(8,128)(2,1)}, bf16[2048,128]{1,0:T(8,128)(2,1)}) custom-call(s32[1]{0:T(128)} %get-tuple-element.44.place_ref, bf16[128,1024]{1,0:T(8,128)(2,1)S(1)} %copy-done.7, f32[16,128]{1,0:T(8,128)S(1)} %get-tuple-element.46.norm_ref, bf16[2048,128]{1,0:T(8,128)(2,1)} %bitcast.4.kv_ref), custom_call_target="tpu_custom_call" | custom-call | flops 1048576 | bytes 65536 | tf_op jit(solution)/shard_map/cond/branch_1_fun/attend/pallas_call | solution.py:259
  53.6 1.6 %collective-permute-done.2.rest_1_ = bf16[192,1024]{1,0:T(8,128)(2,1)} collective-permute-done((bf16[192,1024]{1,0:T(8,128)(2,1)}, bf16[192,1024]{1,0:T(8,128)(2,1)}, u32[]{:S(2)}, u32[]{:S(2)}) %collective-permute-start.2) | collective-permute-done | bytes 393248 | tf_op jit(solution)/shard_map/ppermute | solution.py:38
  55.2 8.8 %collective-permute-done.3.rest_2_ = bf16[192,1024]{1,0:T(8,128)(2,1)} collective-permute-done((bf16[192,1024]{1,0:T(8,128)(2,1)}, bf16[192,1024]{1,0:T(8,128)(2,1)}, u32[]{:S(2)}, u32[]{:S(2)}) %collective-permute-start.3) | collective-permute-done | bytes 393248 | tf_op jit(solution)/shard_map/ppermute | solution.py:38
  64.0 0.0 reduce-scatter.3.cloned.1.call-update
  64.1 0.0 reduce-scatter.5.cloned.1.call-start
  64.1 0.7 reduce-scatter.5.cloned.1.call-update
  64.8 0.0 all-gather.3.cloned.1.call-done
  64.8 0.6 copy-done.2
  65.5 4.3 %back_rows.1 = bf16[512,1024]{1,0:T(8,128)(2,1)} custom-call(s32[1]{0:T(128)} %bitcast.8.line_ref, bf16[512,1536]{1,0:T(8,128)(2,1)S(1)} %bitcast.71, bf16[768,1024]{1,0:T(8,128)(2,1)} %bitcast.72, bf16[192,1024]{1,0:T(8,128)(2,1)} %collective-permute-done.1.rest_0_, bf16[192,1024]{1,0:T(8,128)(2,1)} %collective-permute-done.2.rest_1_, ...), custom_call_target="tpu_custom_call" | custom-call | flops 1048576 | bytes 65536 | tf_op jit(solution)/shard_map/back_rows/pallas_call | solution.py:77
  69.8 0.0 copy-start.10
  69.8 0.0 copy-start.9
  69.8 0.0 copy-start.3
  69.8 0.0 copy-start.5
  69.9 8.5 %all-to-all-start.2 = ((bf16[16,32,1024]{2,1,0:T(8,128)(2,1)}), bf16[16,32,1024]{2,1,0:T(8,128)(2,1)S(1)}, u32[]{:S(2)}, u32[]{:S(2)}) async-start(bf16[16,32,1024]{2,1,0:T(8,128)(2,1)} %bitcast.69), calls=%async_computation.2 | async-start | bytes 2097152 | tf_op jit(solution)/shard_map/all_to_all | solution.py:95
  78.4 0.1 copy.37
  78.5 0.1 eq.33
  78.7 0.2 convert_reduce_fusion
  78.8 0.1 reduce_sum.12
  79.0 0.1 copy.38
  79.1 15.2 %reduce-scatter.3.cloned.1.call-done = bf16[192,1024]{1,0:T(8,128)(2,1)} async-done(((bf16[768,1024]{1,0:T(8,128)(2,1)}), bf16[192,1024]{1,0:T(8,128)(2,1)}) %reduce-scatter.3.cloned.1.call-update) | async-done | bytes 393232 | tf_op jit(solution)/shard_map/reduce_scatter | solution.py:498
  94.2 7.0 %collective-permute-start.5 = (bf16[192,1024]{1,0:T(8,128)(2,1)}, bf16[192,1024]{1,0:T(8,128)(2,1)S(1)}, u32[]{:S(2)}, u32[]{:S(2)}) collective-permute-start(bf16[192,1024]{1,0:T(8,128)(2,1)} %reduce-scatter.3.cloned.1.call-done), channel_id=1, source_target_pairs={{0,256},{64,320},{128,384},{192,448},{256,0},{320,64},{384,128},{4... | collective-permute-start | bytes 1179656 | tf_op jit(solution)/shard_map/ppermute | solution.py:26
  101.3 0.1 iota_compare_fusion
  101.4 0.2 fusion.13
  101.7 4.9 %all-to-all-done.2 = bf16[16,32,1024]{2,1,0:T(8,128)(2,1)S(1)} async-done(((bf16[16,32,1024]{2,1,0:T(8,128)(2,1)}), bf16[16,32,1024]{2,1,0:T(8,128)(2,1)S(1)}, u32[]{:S(2)}, u32[]{:S(2)}) %all-to-all-start.2) | async-done | bytes 1048608 | tf_op jit(solution)/shard_map/all_to_all | solution.py:95
  106.6 34.1 %conditional.5 = (bf16[128,1024]{1,0:T(8,128)(2,1)}, bf16[128,1024]{1,0:T(8,128)(2,1)S(1)}, bf16[2048,128]{1,0:T(8,128)(2,1)}) conditional(s32[]{:T(128)} %convert_element_type.36, () %tuple.35, (bf16[16,32,1024]{2,1,0:T(8,128)(2,1)S(1)}, s32[1]{0:T(128)}, bf16[384,512]{1,0:T(8,128)(2,1)S(1)}, bf16[128,1024]{1,0:T(8,128)(2,1)S(1)}, ...), branch_computations={%region_5.6_spmd, %region_6.7_spmd} | conditional | flops 2097152 | bytes 1703992 | solution.py:364
  106.6 6.2 %key_value_grads.1 = (bf16[128,1024]{1,0:T(8,128)(2,1)}, bf16[2048,128]{1,0:T(8,128)(2,1)}) custom-call(s32[1]{0:T(128)} %get-tuple-element.49.place_ref, bf16[384,512]{1,0:T(8,128)(2,1)S(1)} %get-tuple-element.50.mix_ref, bf16[512,1024]{1,0:T(8,128)(2,1)S(1)} %bitcast.68, bf16[128,1024]{1,0:T(8,128)(2,1)S(1)} %get-tuple-element.148.grad_out_ref, ...), custom_call_target="tpu_custom_call" | custom-call | flops 1048576 | bytes 65536 | tf_op jit(solution)/shard_map/cond/branch_1_fun/key_value_grads/pallas_call | solution.py:259
  112.8 10.4 %all-to-all-start = ((bf16[16,128,128]{2,1,0:T(8,128)(2,1)}), bf16[16,128,128]{2,1,0:T(8,128)(2,1)}, u32[]{:S(2)}, u32[]{:S(2)}) async-start(bf16[16,128,128]{2,1,0:T(8,128)(2,1)} %bitcast.74), calls=%async_computation | async-start | bytes 1048576 | tf_op jit(solution)/shard_map/cond/branch_1_fun/all_to_all | solution.py:95
  123.3 4.5 %query_grads.1 = bf16[128,1024]{1,0:T(8,128)(2,1)S(1)} custom-call(s32[1]{0:T(128)} %get-tuple-element.49.place_ref, bf16[128,1024]{1,0:T(8,128)(2,1)} %get-tuple-element.203.hidden_ref, bf16[128,1024]{1,0:T(8,128)(2,1)S(1)} %get-tuple-element.149.out_ref, bf16[2048,128]{1,0:T(8,128)(2,1)} %get-tuple-element.55.low_ref, ...), custom_call_target="tpu_custom_call" | custom-call | flops 1048576 | bytes 65536 | tf_op jit(solution)/shard_map/cond/branch_1_fun/query_grads/pallas_call | solution.py:259
  127.8 12.9 %all-to-all-done = bf16[16,128,128]{2,1,0:T(8,128)(2,1)} async-done(((bf16[16,128,128]{2,1,0:T(8,128)(2,1)}), bf16[16,128,128]{2,1,0:T(8,128)(2,1)}, u32[]{:S(2)}, u32[]{:S(2)}) %all-to-all-start) | async-done | bytes 524320 | tf_op jit(solution)/shard_map/cond/branch_1_fun/all_to_all | solution.py:95
  140.7 0.8 copy-done.4
  141.5 2.3 %final_sums.1 = (bf16[64,128]{1,0:T(8,128)(2,1)}, bf16[64,128]{1,0:T(8,128)(2,1)}, bf16[192,1024]{1,0:T(8,128)(2,1)}) custom-call(bf16[16,128,128]{2,1,0:T(8,128)(2,1)} %bitcast.23.parts_ref, bf16[192,1024]{1,0:T(8,128)(2,1)} %reduce-scatter.5.cloned.1.call-done.near_ref, bf16[192,1024]{1,0:T(8,128)(2,1)} %copy-done.4), custom_call_target="tpu_custom_call" | custom-call | flops 1048576 | bytes 65536 | tf_op jit(solution)/shard_map/final_sums/pallas_call | solution.py:413
  (27 shorter events, 0.1 us)
Async XLA Ops:
  7.2 57.7 %all-gather.3.cloned.1.call-start = ((), (), s32[]{:S(2)}) async-start(), calls=%async_computation.7 | async-start | bytes 1966080 | tf_op jit(solution)/shard_map/all_gather | solution.py:469
  7.9 25.0 %collective-permute-start.1 = (bf16[192,1024]{1,0:T(8,128)(2,1)}, bf16[192,1024]{1,0:T(8,128)(2,1)}, u32[]{:S(2)}, u32[]{:S(2)}) collective-permute-start(bf16[192,1024]{1,0:T(8,128)(2,1)} %bitcast.75), channel_id=1, source_target_pairs={{0,256},{64,320},{128,384},{192,448},{256,0},{320,64},{384,128},{4... | collective-permute-start | bytes 1179656 | tf_op jit(solution)/shard_map/ppermute | solution.py:26
  16.2 27.3 %copy-start.8 = (f32[16,128]{1,0:T(8,128)S(1)}, f32[16,128]{1,0:T(8,128)}, u32[]{:S(2)}) copy-start(f32[16,128]{1,0:T(8,128)} %param.21) | copy-start | bytes 24580
  22.8 20.7 %copy-start = (bf16[768,1024]{1,0:T(8,128)(2,1)}, bf16[768,1024]{1,0:T(8,128)(2,1)S(1)}, u32[]{:S(2)}) copy-start(bf16[768,1024]{1,0:T(8,128)(2,1)S(1)} %get-tuple-element.113) | copy-start | bytes 4718596
  22.8 20.7 %copy-start.1 = (bf16[768,1024]{1,0:T(8,128)(2,1)}, bf16[768,1024]{1,0:T(8,128)(2,1)S(1)}, u32[]{:S(2)}) copy-start(bf16[768,1024]{1,0:T(8,128)(2,1)S(1)} %get-tuple-element.114) | copy-start | bytes 4718596
  22.8 20.7 %all-to-all-start.1 = ((bf16[8,128,128]{2,1,0:T(8,128)(2,1)}), bf16[8,128,128]{2,1,0:T(8,128)(2,1)S(1)}, u32[]{:S(2)}, u32[]{:S(2)}) async-start(bf16[8,128,128]{2,1,0:T(8,128)(2,1)} %bitcast.11), calls=%async_computation.1 | async-start | bytes 524288 | tf_op jit(solution)/shard_map/all_to_all | solution.py:391
  32.9 61.4 %reduce-scatter.3.cloned.1.call-start = ((), (), s32[]{:S(2)}) async-start(), calls=%async_computation.5 | async-start | bytes 1966080 | tf_op jit(solution)/shard_map/reduce_scatter | solution.py:498
  32.9 22.3 %collective-permute-start.2 = (bf16[192,1024]{1,0:T(8,128)(2,1)}, bf16[192,1024]{1,0:T(8,128)(2,1)}, u32[]{:S(2)}, u32[]{:S(2)}) collective-permute-start(bf16[192,1024]{1,0:T(8,128)(2,1)} %collective-permute-done.1.rest_0_), channel_id=1, source_target_pairs={{0,64},{64,128},{128,192},{192,0},{256,320},{320,384},{384,448},{4... | collective-permute-start | bytes 1179656 | tf_op jit(solution)/shard_map/ppermute | solution.py:38
  36.0 28.0 %collective-permute-start.3 = (bf16[192,1024]{1,0:T(8,128)(2,1)}, bf16[192,1024]{1,0:T(8,128)(2,1)}, u32[]{:S(2)}, u32[]{:S(2)}) collective-permute-start(bf16[192,1024]{1,0:T(8,128)(2,1)} %collective-permute-done.1.rest_0_), channel_id=1, source_target_pairs={{0,128},{64,192},{128,0},{192,64},{256,384},{320,448},{384,256},{4... | collective-permute-start | bytes 1179656 | tf_op jit(solution)/shard_map/ppermute | solution.py:38
  40.4 23.6 %collective-permute-start.4 = (bf16[192,1024]{1,0:T(8,128)(2,1)}, bf16[192,1024]{1,0:T(8,128)(2,1)}, u32[]{:S(2)}, u32[]{:S(2)}) collective-permute-start(bf16[192,1024]{1,0:T(8,128)(2,1)} %collective-permute-done.1.rest_0_), channel_id=1, source_target_pairs={{0,192},{64,0},{128,64},{192,128},{256,448},{320,256},{384,320},{4... | collective-permute-start | bytes 1179656 | tf_op jit(solution)/shard_map/ppermute | solution.py:38
  43.5 5.2 %collective-permute-start = (bf16[1024,128]{1,0:T(8,128)(2,1)S(1)}, bf16[1024,128]{1,0:T(8,128)(2,1)S(1)}, u32[]{:S(2)}, u32[]{:S(2)}) collective-permute-start(bf16[1024,128]{1,0:T(8,128)(2,1)S(1)} %bitcast.73), channel_id=1, source_target_pairs={{0,4},{4,0},{8,12},{12,8},{16,20},{20,16},{24,28},{28,24},{32,36},... | collective-permute-start | bytes 786440 | tf_op jit(solution)/shard_map/cond/branch_1_fun/ppermute | solution.py:396
  48.8 1.0 copy-start.7
  64.0 1.4 copy-start.2
  64.1 76.6 %reduce-scatter.5.cloned.1.call-start = ((), (), s32[]{:S(2)}) async-start(), calls=%async_computation.6 | async-start | bytes 1966080 | tf_op jit(solution)/shard_map/reduce_scatter | solution.py:498
  69.8 8.5 %copy-start.10 = (f32[128,2]{0,1:T(2,128)S(1)}, f32[128,2]{0,1:T(2,128)}, u32[]{:S(2)}) copy-start(f32[128,2]{0,1:T(2,128)} %param.24) | copy-start | bytes 3076
  69.8 8.6 %copy-start.9 = (s32[128,2]{0,1:T(2,128)S(1)}, s32[128,2]{0,1:T(2,128)}, u32[]{:S(2)}) copy-start(s32[128,2]{0,1:T(2,128)} %param.23) | copy-start | bytes 3076
  69.8 36.7 %copy-start.3 = (bf16[128,1024]{1,0:T(8,128)(2,1)S(1)}, bf16[128,1024]{1,0:T(8,128)(2,1)}, u32[]{:S(2)}) copy-start(bf16[128,1024]{1,0:T(8,128)(2,1)} %param.20) | copy-start | bytes 786436
  69.8 36.7 %copy-start.5 = (bf16[128,1024]{1,0:T(8,128)(2,1)S(1)}, bf16[128,1024]{1,0:T(8,128)(2,1)}, u32[]{:S(2)}) copy-start(bf16[128,1024]{1,0:T(8,128)(2,1)} %param.22) | copy-start | bytes 786436
  69.9 36.7 %all-to-all-start.2 = ((bf16[16,32,1024]{2,1,0:T(8,128)(2,1)}), bf16[16,32,1024]{2,1,0:T(8,128)(2,1)S(1)}, u32[]{:S(2)}, u32[]{:S(2)}) async-start(bf16[16,32,1024]{2,1,0:T(8,128)(2,1)} %bitcast.69), calls=%async_computation.2 | async-start | bytes 2097152 | tf_op jit(solution)/shard_map/all_to_all | solution.py:95
  94.2 46.5 %collective-permute-start.5 = (bf16[192,1024]{1,0:T(8,128)(2,1)}, bf16[192,1024]{1,0:T(8,128)(2,1)S(1)}, u32[]{:S(2)}, u32[]{:S(2)}) collective-permute-start(bf16[192,1024]{1,0:T(8,128)(2,1)} %reduce-scatter.3.cloned.1.call-done), channel_id=1, source_target_pairs={{0,256},{64,320},{128,384},{192,448},{256,0},{320,64},{384,128},{4... | collective-permute-start | bytes 1179656 | tf_op jit(solution)/shard_map/ppermute | solution.py:26
  112.8 27.9 %all-to-all-start = ((bf16[16,128,128]{2,1,0:T(8,128)(2,1)}), bf16[16,128,128]{2,1,0:T(8,128)(2,1)}, u32[]{:S(2)}, u32[]{:S(2)}) async-start(bf16[16,128,128]{2,1,0:T(8,128)(2,1)} %bitcast.74), calls=%async_computation | async-start | bytes 1048576 | tf_op jit(solution)/shard_map/cond/branch_1_fun/all_to_all | solution.py:95
  140.7 3.1 %copy-start.6 = (bf16[128,1024]{1,0:T(8,128)(2,1)}, bf16[128,1024]{1,0:T(8,128)(2,1)S(1)}, u32[]{:S(2)}) copy-start(bf16[128,1024]{1,0:T(8,128)(2,1)S(1)} %get-tuple-element.89) | copy-start | bytes 786436
  140.7 0.8 copy-start.4
Sparse Core Ops, SparseCore 0:
  10.1 45.0 all-gather.2
  64.2 30.0 reduce-scatter.2
  97.1 30.7 reduce-scatter.4
